TPU v7x, 512 devices: a whole 4x4x16 slice. The times are simulated.
512 devices in a mesh: gx: 32 (over x, z_lo, core), gy: 16 (over z_hi, y).
Axes of the slice: x: 4, y: 4, z: 16 (z_hi: 4, z_lo: 4; z = z_hi * 4 + z_lo), core: 2. Of those that a mesh axis runs over, the one named last changes fastest.
Arguments:
- sky_image: float32 [4096, 4096], P('gx', 'gy'), may hold values from -6 to 6
- visibilities: bfloat16 [32, 16, 64, 2, 64], P('gx', 'gy'), may hold values from -6 to 6
- grid_kernels: bfloat16 [32, 16, 64, 64, 256], P('gx', 'gy'), may hold values from -0.75 to 0.75
- tile_counts: int32 [32, 16, 128], P('gx', 'gy'), may hold values from 0 to 16, as said below
- block_tiles: int32 [32, 16, 64], P('gx', 'gy'), may hold values from 0 to 127, as said below
- enter_weight: bfloat16 [3, 3, 32, 2], replicated, may hold values from -2 to 2
- enter_bias: float32 [32], replicated, may hold values from -3 to 3
- encode_weight: bfloat16 [3, 3, 32, 32], replicated, may hold values from -0.5 to 0.5
- encode_bias: float32 [32], replicated, may hold values from -3 to 3
- coarse_weight: bfloat16 [3, 3, 64, 32], replicated, may hold values from -0.5 to 0.5
- coarse_bias: float32 [64], replicated, may hold values from -3 to 3
- deeper_weight: bfloat16 [3, 3, 64, 64], replicated, may hold values from -0.375 to 0.375
- deeper_bias: float32 [64], replicated, may hold values from -3 to 3
- upward_weight: bfloat16 [32, 64], replicated, may hold values from -0.75 to 0.75
- skip_weight: bfloat16 [32, 32], replicated, may hold values from -1 to 1
- merge_bias: float32 [32], replicated, may hold values from -3 to 3
- decode_weight: bfloat16 [3, 3, 32, 32], replicated, may hold values from -0.5 to 0.5
- decode_bias: float32 [32], replicated, may hold values from -3 to 3
- output_weight: bfloat16 [3, 3, 1, 32], replicated, may hold values from -0.375 to 0.375
Outputs:
- dirty_image: float32 [4096, 4096], P('gx', 'gy')
- estimate: float32 [4096, 4096], P('gx', 'gy')
Inputs may be any that keep to these rules, and one draw needn't show every extreme that they name: `tile_counts`: on each device the live blocks (the sum of its tile counts) number 1 to 64; the devices at the centre of the uv plane hold exactly 64, and the load falls away from the centre. No tile holds more than 16 blocks, and some tile of a centre device holds exactly that many. `block_tiles`: the first L slots of a device (L the sum of its tile counts) name their tiles in non-decreasing order, tile t as often as its count; the remaining slots hold 0 and carry no data.
All inputs are finite; a program needn't handle non-finite values.
Results may differ from a plain program's by a relative error of at most 0.015.
Values may be sent and summed in bfloat16 or wider, within the bound.
A program may use at most 128 MiB of HBM per device.

v0:
```python
import math

import jax
import jax.numpy as jnp
from jax import lax
from jax.sharding import PartitionSpec as P

TILE_R = 8
TILE_C = 32


full_turn = 2.0 * math.pi


def padded_2(array, sides, width):
    for axis, dim in sides:
        peers, length = (lax.axis_size(axis), array.shape[dim])
        up = [(i, (i + 1) % peers) for i in range(peers - 1)]
        down = [(j, i) for i, j in up]
        last = lax.slice_in_dim(array, length - width, length, axis=dim)
        initial = lax.slice_in_dim(array, 0, width, axis=dim)
        before = lax.ppermute(last, axis, up)
        after = lax.ppermute(initial, axis, down)
        array = jnp.concatenate([before, array, after], axis=dim)
    return array


def conv_valid(padded, weight, bias_vec):
    out_rows = padded.shape[1] - 2
    out_cols = padded.shape[2] - 2
    summed = None
    for row_shift in range(3):
        for col_shift in range(3):
            window = padded[:, row_shift : row_shift + out_rows, col_shift : col_shift + out_cols]
            tap_term = jnp.einsum(
                "oc,chw->ohw",
                weight[row_shift, col_shift],
                window,
                preferred_element_type=jnp.float32,
            )
            summed = tap_term if summed is None else summed + tap_term
    return summed + bias_vec[:, None, None]


def fine_conv(values, weight, bias_vec):
    padded = padded_2(values, (("gx", 1), ("gy", 2)), 1)
    return conv_valid(padded, weight, bias_vec)


def coarse_conv(values, weight, bias_vec):
    padded = padded_2(values, (("gx", 1), ("gy", 2)), 1)
    return conv_valid(padded, weight, bias_vec)


def angle_table(first_ids, second_ids, period):
    phases = (first_ids[:, None] * second_ids[None, :] % period).astype(jnp.float32) * (
        full_turn / period
    )
    return (jnp.cos(phases), jnp.sin(phases))


def dft_axis(planes, inner_len, outer_len, real_only):
    highest = lax.Precision.HIGHEST
    line_count = planes.shape[1]
    real_part = planes[0].reshape(line_count, inner_len, outer_len)
    imag_part = planes[1].reshape(line_count, inner_len, outer_len)
    inner_ids = jnp.arange(inner_len, dtype=jnp.int32)
    outer_ids = jnp.arange(outer_len, dtype=jnp.int32)
    inner_cos, inner_sin = angle_table(inner_ids, inner_ids, inner_len)
    first_real = jnp.einsum("mab,ay->myb", real_part, inner_cos, precision=highest) - jnp.einsum(
        "mab,ay->myb", imag_part, inner_sin, precision=highest
    )
    first_imag = jnp.einsum("mab,ay->myb", real_part, inner_sin, precision=highest) + jnp.einsum(
        "mab,ay->myb", imag_part, inner_cos, precision=highest
    )
    twist_cos, twist_sin = angle_table(inner_ids, outer_ids, inner_len * outer_len)
    second_real = first_real * twist_cos[None] - first_imag * twist_sin[None]
    second_imag = first_real * twist_sin[None] + first_imag * twist_cos[None]
    outer_cos, outer_sin = angle_table(outer_ids, outer_ids, outer_len)
    final_real = jnp.einsum("myb,bz->mzy", second_real, outer_cos, precision=highest) - jnp.einsum(
        "myb,bz->mzy", second_imag, outer_sin, precision=highest
    )
    if real_only:
        return final_real.reshape(line_count, inner_len * outer_len)
    final_imag = jnp.einsum("myb,bz->mzy", second_real, outer_sin, precision=highest) + jnp.einsum(
        "myb,bz->mzy", second_imag, outer_cos, precision=highest
    )
    return jnp.stack([final_real, final_imag]).reshape(2, line_count, inner_len * outer_len)


def shards(
    sky_image,
    visibilities,
    grid_kernels,
    tile_counts,
    block_tiles,
    enter_weight,
    enter_bias,
    encode_weight,
    encode_bias,
    coarse_weight,
    coarse_bias,
    deeper_weight,
    deeper_bias,
    upward_weight,
    skip_weight,
    merge_bias,
    decode_weight,
    decode_bias,
    output_weight,
):
    row_count, col_count = sky_image.shape
    row_devices = lax.axis_size("gx")
    col_devices = lax.axis_size("gy")
    total_rows = row_count * row_devices
    total_cols = col_count * col_devices
    slot_count = block_tiles.shape[2]
    tile_count = tile_counts.shape[2]
    visible = visibilities[0, 0]
    kernels = grid_kernels[0, 0]
    cell_count = kernels.shape[2]
    owners = block_tiles[0, 0]
    live_blocks = jnp.sum(tile_counts[0, 0])
    contrib = jnp.einsum("bkv,bvc->bkc", visible, kernels, preferred_element_type=jnp.float32)
    contrib = contrib.reshape(slot_count, 2 * cell_count)
    living = jnp.arange(slot_count, dtype=jnp.int32) < live_blocks
    onehot = (owners[None, :] == jnp.arange(tile_count, dtype=jnp.int32)[:, None]) & living[None, :]
    tile_sums = jnp.dot(onehot.astype(jnp.float32), contrib, precision=lax.Precision.HIGHEST)
    uv_grid = tile_sums.reshape(row_count // TILE_R, col_count // TILE_C, 2, TILE_R, TILE_C)
    uv_grid = uv_grid.transpose(2, 0, 3, 1, 4).reshape(2, row_count, col_count)
    spread = lax.all_to_all(
        uv_grid.astype(jnp.bfloat16), "gy", split_axis=1, concat_axis=2, tiled=True
    ).astype(uv_grid.dtype)
    spread = dft_axis(spread, col_count, col_devices, False)
    partial_value = lax.all_to_all(
        spread.astype(jnp.bfloat16), "gy", split_axis=2, concat_axis=1, tiled=True
    ).astype(spread.dtype)
    turned = jnp.swapaxes(partial_value, 1, 2)
    across = lax.all_to_all(
        turned.astype(jnp.bfloat16), "gx", split_axis=1, concat_axis=2, tiled=True
    ).astype(turned.dtype)
    real_rows = dft_axis(across, row_count, row_devices, True)
    raw_image = (
        lax.all_to_all(
            real_rows.astype(jnp.bfloat16), "gx", split_axis=1, concat_axis=0, tiled=True
        )
        .astype(real_rows.dtype)
        .T
    )
    global_rows = lax.axis_index("gx") * row_count + jnp.arange(row_count, dtype=jnp.int32)
    global_cols = lax.axis_index("gy") * col_count + jnp.arange(col_count, dtype=jnp.int32)
    parity = (1 - 2 * ((global_rows[:, None] + global_cols[None, :]) % 2)).astype(jnp.float32)
    dirty_image = raw_image * parity * (1.0 / math.sqrt(total_rows * total_cols))
    net_input = jnp.stack([sky_image, dirty_image]).astype(jnp.bfloat16)
    padded = padded_2(net_input, (("gx", 1), ("gy", 2)), 1)
    entered = jax.nn.relu(conv_valid(padded, enter_weight, enter_bias)).astype(jnp.bfloat16)
    encoded = jax.nn.relu(fine_conv(entered, encode_weight, encode_bias)).astype(jnp.bfloat16)
    pooled = (
        encoded[:, 0::2, 0::2].astype(jnp.float32)
        + encoded[:, 1::2, 0::2].astype(jnp.float32)
        + encoded[:, 0::2, 1::2].astype(jnp.float32)
        + encoded[:, 1::2, 1::2].astype(jnp.float32)
    )
    pooled = (pooled * 0.25).astype(jnp.bfloat16)
    coarse = jax.nn.relu(coarse_conv(pooled, coarse_weight, coarse_bias)).astype(jnp.bfloat16)
    deeper = jax.nn.relu(coarse_conv(coarse, deeper_weight, deeper_bias)).astype(jnp.bfloat16)
    lifted = jnp.einsum("oc,chw->ohw", upward_weight, deeper, preferred_element_type=jnp.float32)
    lifted = jnp.repeat(jnp.repeat(lifted, 2, axis=1), 2, axis=2)
    joined = lifted + jnp.einsum(
        "oc,chw->ohw", skip_weight, encoded, preferred_element_type=jnp.float32
    )
    merged = jax.nn.relu(joined + merge_bias[:, None, None]).astype(jnp.bfloat16)
    decoded = jax.nn.relu(fine_conv(merged, decode_weight, decode_bias)).astype(jnp.bfloat16)
    update = fine_conv(decoded, output_weight, jnp.zeros((1,), jnp.float32))
    estimate = sky_image + update[0]
    return (dirty_image, estimate)


def solution(mesh):
    return jax.shard_map(
        shards,
        mesh=mesh,
        in_specs=(
            P("gx", "gy"),
            P("gx", "gy", None, None, None),
            P("gx", "gy", None, None, None),
            P("gx", "gy", None),
            P("gx", "gy", None),
            P(),
            P(),
            P(),
            P(),
            P(),
            P(),
            P(),
            P(),
            P(),
            P(),
            P(),
            P(),
            P(),
            P(),
        ),
        out_specs=(P("gx", "gy"), P("gx", "gy")),
        check_vma=False,
    )
```

profile of v0, /device:TPU:130, one launch (start us, length us, event | category | flops | bytes accessed | tf_op | source)
XLA Modules:
  0.0 562.9 jit_solution(11381955879651305043)
XLA Ops:
  6.2 16.5 %all-to-all-start = ((bf16[2,128,256]{2,0,1:T(2,128)(2,1)}), bf16[2,128,256]{2,0,1:T(2,128)(2,1)S(1)}, u32[]{:S(2)}, u32[]{:S(2)}) async-start(bf16[2,128,256]{2,0,1:T(2,128)(2,1)} %reshape.311), calls=%async_computation | async-start | bytes 262144 | tf_op jit(solution)/shard_map/all_to_all | solution.py:131
  22.8 12.0 %all-to-all-done = bf16[2,128,256]{2,0,1:T(2,128)(2,1)S(1)} async-done(((bf16[2,128,256]{2,0,1:T(2,128)(2,1)}), bf16[2,128,256]{2,0,1:T(2,128)(2,1)S(1)}, u32[]{:S(2)}, u32[]{:S(2)}) %all-to-all-start) | async-done | bytes 131104 | tf_op jit(solution)/shard_map/all_to_all | solution.py:131
  47.3 18.5 %all_to_all.49 = bf16[16,2,2048]{2,1,0:T(2,128)(2,1)S(1)} all-to-all(bf16[16,2,2048]{2,1,0:T(2,128)(2,1)S(1)} %reshape.312), channel_id=1, replica_groups=mesh['gx'=32,'gy'=16] {'gy'}, dimensions={0} | all-to-all | bytes 262144 | tf_op jit(solution)/shard_map/all_to_all | solution.py:135
  70.3 8.6 %all-to-all-start.2 = ((bf16[2,256,128]{2,0,1:T(2,128)(2,1)}), bf16[2,256,128]{2,0,1:T(2,128)(2,1)S(1)}, u32[]{:S(2)}, u32[]{:S(2)}) async-start(bf16[2,256,128]{2,0,1:T(2,128)(2,1)} %copy.167), calls=%async_computation.2 | async-start | bytes 262144 | tf_op jit(solution)/shard_map/all_to_all | solution.py:139
  79.0 7.5 %all-to-all-done.2 = bf16[2,256,128]{2,0,1:T(2,128)(2,1)S(1)} async-done(((bf16[2,256,128]{2,0,1:T(2,128)(2,1)}), bf16[2,256,128]{2,0,1:T(2,128)(2,1)S(1)}, u32[]{:S(2)}, u32[]{:S(2)}) %all-to-all-start.2) | async-done | bytes 131104 | tf_op jit(solution)/shard_map/all_to_all | solution.py:139
  90.5 5.0 all-to-all-start.3
  95.6 6.7 %all-to-all-done.3 = bf16[8,32,128]{2,0,1:T(8,128)(2,1)S(1)} async-done(((bf16[8,32,128]{2,0,1:T(8,128)(2,1)}), bf16[8,32,128]{2,0,1:T(8,128)(2,1)S(1)}, u32[]{:S(2)}, u32[]{:S(2)}) %all-to-all-start.3) | async-done | bytes 65568 | tf_op jit(solution)/shard_map/all_to_all | solution.py:144
  104.6 6.3 %collective-permute-start.1 = (bf16[2,1,256]{2,0,1:T(2,128)(2,1)S(1)}, bf16[2,1,256]{2,0,1:T(2,128)(2,1)S(1)}, u32[]{:S(2)}, u32[]{:S(2)}) collective-permute-start(bf16[2,1,256]{2,0,1:T(2,128)(2,1)S(1)} %get-tuple-element.49), channel_id=1, source_target_pairs={{16,0},{32,16},{48,32},{64,48},{80,64},{96,80},{112,96},{128,112},... | collective-permute-start | bytes 3080 | tf_op jit(solution)/shard_map/ppermute | solution.py:23
  115.0 7.8 %collective-permute-start.3 = (bf16[2,130,1]{2,0,1:T(2,128)(2,1)S(1)}, bf16[2,130,1]{2,0,1:T(2,128)(2,1)S(1)}, u32[]{:S(2)}, u32[]{:S(2)}) collective-permute-start(bf16[2,130,1]{2,0,1:T(2,128)(2,1)S(1)} %get-tuple-element.50), channel_id=1, source_target_pairs={{1,0},{2,1},{3,2},{4,3},{5,4},{6,5},{7,6},{8,7},{9,8},{10,9},{11,1... | collective-permute-start | bytes 1568 | tf_op jit(solution)/shard_map/ppermute | solution.py:23
  126.3 8.7 %collective-permute-done.2 = bf16[2,130,1]{2,0,1:T(2,128)(2,1)S(1)} collective-permute-done((bf16[2,130,1]{2,0,1:T(2,128)(2,1)S(1)}, bf16[2,130,1]{2,0,1:T(2,128)(2,1)S(1)}, u32[]{:S(2)}, u32[]{:S(2)}) %collective-permute-start.2) | collective-permute-done | bytes 552 | tf_op jit(solution)/shard_map/ppermute | solution.py:22
  150.6 8.7 %fusion.61 = bf16[32,128,256]{2,0,1:T(8,128)(2,1)S(1)} fusion(f32[32]{0:T(128)S(1)} %copy-done.27, f32[128,256,32]{1,2,0:T(8,128)S(1)} %fusion.135, f32[128,256,32]{1,2,0:T(8,128)} %fusion.151, f32[128,256,32]{1,2,0:T(8,128)} %fusion.153, f32[128,256,32]{1,2,0:T(8,128)S(1)} %copy-done.5, f32[128,256,32]{1,2,0:T(8,128)} %fusion.155, ...), kind=kOutput, calls=%fused_computation.78 | convolution fusion | flops 15728640 | bytes 35783680 | tf_op jit(solution)/shard_map/oc,chw->ohw/dot_general | solution.py:35
  161.2 6.5 %collective-permute-start.5 = (bf16[32,1,256]{2,0,1:T(8,128)(2,1)S(1)}, bf16[32,1,256]{2,0,1:T(8,128)(2,1)S(1)}, u32[]{:S(2)}, u32[]{:S(2)}) collective-permute-start(bf16[32,1,256]{2,0,1:T(8,128)(2,1)S(1)} %get-tuple-element.31), channel_id=1, source_target_pairs={{16,0},{32,16},{48,32},{64,48},{80,64},{96,80},{112,96},{128,112},... | collective-permute-start | bytes 49160 | tf_op jit(solution)/shard_map/ppermute | solution.py:23
  194.2 5.2 maximum_maximum_fusion
  213.4 10.9 %fusion.62 = bf16[32,128,256]{2,0,1:T(8,128)(2,1)S(1)} fusion(f32[32]{0:T(128)S(1)} %copy-done.28, bf16[32,130,257]{2,0,1:T(8,128)(2,1)S(1)} %get-tuple-element.23, f32[128,256,32]{1,2,0:T(8,128)} %fusion.45, f32[128,256,32]{1,2,0:T(8,128)} %fusion.47, f32[128,256,32]{1,2,0:T(8,128)} %fusion.49, f32[128,256,32]{1,2,0:T(8,128)S(1)} %copy-done.3, ...), kind=kOutput, calls=%fused_computation.79 | convolution fusion | flops 78643200 | bytes 37757440 | tf_op jit(solution)/shard_map/oc,chw->ohw/dot_general | solution.py:35
  224.3 23.4 %slice.503 = bf16[32,64,128]{2,0,1:T(8,128)(2,1)S(1)} slice(bf16[32,128,256]{2,0,1:T(8,128)(2,1)S(1)} %fusion.62), slice={[0:32:1], [1:128:2], [1:256:2]} | slice | bytes 1048576 | tf_op jit(solution)/shard_map/slice | solution.py:162
  247.8 22.7 %slice.502 = bf16[32,64,128]{2,0,1:T(8,128)(2,1)S(1)} slice(bf16[32,128,256]{2,0,1:T(8,128)(2,1)S(1)} %fusion.62), slice={[0:32:1], [0:128:2], [1:256:2]} | slice | bytes 1048576 | tf_op jit(solution)/shard_map/slice | solution.py:161
  270.5 30.5 %slice.501 = bf16[32,64,128]{2,0,1:T(8,128)(2,1)} slice(bf16[32,128,256]{2,0,1:T(8,128)(2,1)S(1)} %fusion.62), slice={[0:32:1], [1:128:2], [0:256:2]} | slice | bytes 1048576 | tf_op jit(solution)/shard_map/slice | solution.py:160
  301.0 30.5 %slice.500 = bf16[32,64,128]{2,0,1:T(8,128)(2,1)} slice(bf16[32,128,256]{2,0,1:T(8,128)(2,1)S(1)} %fusion.62), slice={[0:32:1], [0:128:2], [0:256:2]} | slice | bytes 1048576 | tf_op jit(solution)/shard_map/slice | solution.py:159
  334.9 6.7 %collective-permute-start.9 = (bf16[32,1,128]{2,0,1:T(8,128)(2,1)S(1)}, bf16[32,1,128]{2,0,1:T(8,128)(2,1)S(1)}, u32[]{:S(2)}, u32[]{:S(2)}) collective-permute-start(bf16[32,1,128]{2,0,1:T(8,128)(2,1)S(1)} %get-tuple-element.45), channel_id=1, source_target_pairs={{16,0},{32,16},{48,32},{64,48},{80,64},{96,80},{112,96},{128,112},... | collective-permute-start | bytes 24584 | tf_op jit(solution)/shard_map/ppermute | solution.py:23
  347.1 9.9 %collective-permute-start.11 = (bf16[32,66,1]{1,0,2:T(8,128)(2,1)S(1)}, bf16[32,66,1]{1,0,2:T(8,128)(2,1)S(1)}, u32[]{:S(2)}, u32[]{:S(2)}) collective-permute-start(bf16[32,66,1]{1,0,2:T(8,128)(2,1)S(1)} %copy.185), channel_id=1, source_target_pairs={{1,0},{2,1},{3,2},{4,3},{5,4},{6,5},{7,6},{8,7},{9,8},{10,9},{11,1... | collective-permute-start | bytes 12680 | tf_op jit(solution)/shard_map/ppermute | solution.py:23
  370.8 6.3 %collective-permute-start.13 = (bf16[64,1,128]{2,0,1:T(8,128)(2,1)S(1)}, bf16[64,1,128]{2,0,1:T(8,128)(2,1)S(1)}, u32[]{:S(2)}, u32[]{:S(2)}) collective-permute-start(bf16[64,1,128]{2,0,1:T(8,128)(2,1)S(1)} %get-tuple-element.37), channel_id=1, source_target_pairs={{16,0},{32,16},{48,32},{64,48},{80,64},{96,80},{112,96},{128,112},... | collective-permute-start | bytes 49160 | tf_op jit(solution)/shard_map/ppermute | solution.py:23
  384.4 7.9 %collective-permute-start.15 = (bf16[64,66,1]{1,0,2:T(8,128)(2,1)S(1)}, bf16[64,66,1]{1,0,2:T(8,128)(2,1)S(1)}, u32[]{:S(2)}, u32[]{:S(2)}) collective-permute-start(bf16[64,66,1]{1,0,2:T(8,128)(2,1)S(1)} %copy.189), channel_id=1, source_target_pairs={{1,0},{2,1},{3,2},{4,3},{5,4},{6,5},{7,6},{8,7},{9,8},{10,9},{11,1... | collective-permute-start | bytes 25352 | tf_op jit(solution)/shard_map/ppermute | solution.py:23
  398.0 5.9 %collective-permute-done.14 = bf16[64,66,1]{1,0,2:T(8,128)(2,1)S(1)} collective-permute-done((bf16[64,66,1]{1,0,2:T(8,128)(2,1)S(1)}, bf16[64,66,1]{1,0,2:T(8,128)(2,1)S(1)}, u32[]{:S(2)}, u32[]{:S(2)}) %collective-permute-start.14) | collective-permute-done | bytes 8480 | tf_op jit(solution)/shard_map/ppermute | solution.py:22
  421.9 7.5 %convolution_bitcast_fusion = f32[32,64,128]{2,0,1:T(8,128)S(1)} fusion(bf16[64,66,129]{2,0,1:T(8,128)(2,1)} %copy-done.6, f32[64,128,64]{1,2,0:T(8,128)} %fusion.84, f32[64,128,64]{1,2,0:T(8,128)} %fusion.86, f32[64,128,64]{1,2,0:T(8,128)} %fusion.88, f32[64,128,64]{1,2,0:T(8,128)S(1)} %copy-done.10, f32[64,128,64]{1,2,0:T(8,128)} %fusion.90, ...), kind=kOutput, calls=%fused_computation.81 | convolution fusion | flops 106430464 | bytes 18895104 | tf_op jit(solution)/shard_map/oc,chw->ohw/dot_general | solution.py:167
  436.3 5.6 %copy.192 = f32[32,128,256]{2,0,1:T(8,128)} copy(f32[32,128,256]{1,0,2:T(8,128)} %bitcast.478) | data formatting | bytes 8388608 | tf_op jit(solution)/shard_map/reshape | solution.py:168
  447.4 6.7 %collective-permute-start.17 = (bf16[32,1,256]{2,0,1:T(8,128)(2,1)S(1)}, bf16[32,1,256]{2,0,1:T(8,128)(2,1)S(1)}, u32[]{:S(2)}, u32[]{:S(2)}) collective-permute-start(bf16[32,1,256]{2,0,1:T(8,128)(2,1)S(1)} %get-tuple-element.29), channel_id=1, source_target_pairs={{16,0},{32,16},{48,32},{64,48},{80,64},{96,80},{112,96},{128,112},... | collective-permute-start | bytes 49160 | tf_op jit(solution)/shard_map/ppermute | solution.py:23
  482.8 5.2 maximum_maximum_fusion.1
  502.0 10.9 %fusion.65 = bf16[32,128,256]{2,0,1:T(8,128)(2,1)S(1)} fusion(f32[32]{0:T(128)S(1)} %copy-done.29, bf16[32,130,257]{2,0,1:T(8,128)(2,1)S(1)} %get-tuple-element.19, f32[128,256,32]{1,2,0:T(8,128)} %fusion.27, f32[128,256,32]{1,2,0:T(8,128)} %fusion.29, f32[128,256,32]{1,2,0:T(8,128)} %fusion.31, f32[128,256,32]{1,2,0:T(8,128)S(1)} %copy-done.4, ...), kind=kOutput, calls=%fused_computation.80 | convolution fusion | flops 78643200 | bytes 37757440 | tf_op jit(solution)/shard_map/oc,chw->ohw/dot_general | solution.py:35
  514.8 6.5 %collective-permute-start.21 = (bf16[32,1,256]{2,0,1:T(8,128)(2,1)S(1)}, bf16[32,1,256]{2,0,1:T(8,128)(2,1)S(1)}, u32[]{:S(2)}, u32[]{:S(2)}) collective-permute-start(bf16[32,1,256]{2,0,1:T(8,128)(2,1)S(1)} %get-tuple-element.27), channel_id=1, source_target_pairs={{16,0},{32,16},{48,32},{64,48},{80,64},{96,80},{112,96},{128,112},... | collective-permute-start | bytes 49160 | tf_op jit(solution)/shard_map/ppermute | solution.py:23
  529.5 5.8 %collective-permute-start.23 = (bf16[32,130,1]{1,0,2:T(8,128)(2,1)}, bf16[32,130,1]{1,0,2:T(8,128)(2,1)}, u32[]{:S(2)}, u32[]{:S(2)}) collective-permute-start(bf16[32,130,1]{1,0,2:T(8,128)(2,1)} %copy.199), channel_id=1, source_target_pairs={{1,0},{2,1},{3,2},{4,3},{5,4},{6,5},{7,6},{8,7},{9,8},{10,9},{11,1... | collective-permute-start | bytes 24968 | tf_op jit(solution)/shard_map/ppermute | solution.py:23
  540.0 7.2 %collective-permute-done.22 = bf16[32,130,1]{1,0,2:T(8,128)(2,1)} collective-permute-done((bf16[32,130,1]{1,0,2:T(8,128)(2,1)}, bf16[32,130,1]{1,0,2:T(8,128)(2,1)}, u32[]{:S(2)}, u32[]{:S(2)}) %collective-permute-start.22) | collective-permute-done | bytes 8352 | tf_op jit(solution)/shard_map/ppermute | solution.py:22
  553.3 4.9 maximum_maximum_fusion.2
  (250 shorter events, 227.9 us)
Async XLA Ops:
  6.2 28.5 %all-to-all-start = ((bf16[2,128,256]{2,0,1:T(2,128)(2,1)}), bf16[2,128,256]{2,0,1:T(2,128)(2,1)S(1)}, u32[]{:S(2)}, u32[]{:S(2)}) async-start(bf16[2,128,256]{2,0,1:T(2,128)(2,1)} %reshape.311), calls=%async_computation | async-start | bytes 262144 | tf_op jit(solution)/shard_map/all_to_all | solution.py:131
  70.3 16.2 %all-to-all-start.2 = ((bf16[2,256,128]{2,0,1:T(2,128)(2,1)}), bf16[2,256,128]{2,0,1:T(2,128)(2,1)S(1)}, u32[]{:S(2)}, u32[]{:S(2)}) async-start(bf16[2,256,128]{2,0,1:T(2,128)(2,1)} %copy.167), calls=%async_computation.2 | async-start | bytes 262144 | tf_op jit(solution)/shard_map/all_to_all | solution.py:139
  87.8 23.1 %copy-start.22 = (bf16[3,3,32,2]{2,3,1,0:T(2,128)(2,1)S(1)}, bf16[3,3,32,2]{2,3,1,0:T(2,128)(2,1)}, u32[]{:S(2)}) copy-start(bf16[3,3,32,2]{2,3,1,0:T(2,128)(2,1)} %param.24) | copy-start | bytes 3460
  90.5 11.9 %all-to-all-start.3 = ((bf16[8,32,128]{2,0,1:T(8,128)(2,1)}), bf16[8,32,128]{2,0,1:T(8,128)(2,1)S(1)}, u32[]{:S(2)}, u32[]{:S(2)}) async-start(bf16[8,32,128]{2,0,1:T(8,128)(2,1)} %copy.175), calls=%async_computation.3 | async-start | bytes 131072 | tf_op jit(solution)/shard_map/all_to_all | solution.py:144
  102.6 11.9 %collective-permute-start = (bf16[2,1,256]{2,0,1:T(2,128)(2,1)S(1)}, bf16[2,1,256]{2,0,1:T(2,128)(2,1)S(1)}, u32[]{:S(2)}, u32[]{:S(2)}) collective-permute-start(bf16[2,1,256]{2,0,1:T(2,128)(2,1)S(1)} %get-tuple-element.48), channel_id=1, source_target_pairs={{0,16},{16,32},{32,48},{48,64},{64,80},{80,96},{96,112},{112,128},... | collective-permute-start | bytes 3080 | tf_op jit(solution)/shard_map/ppermute | solution.py:22
  104.6 10.0 %collective-permute-start.1 = (bf16[2,1,256]{2,0,1:T(2,128)(2,1)S(1)}, bf16[2,1,256]{2,0,1:T(2,128)(2,1)S(1)}, u32[]{:S(2)}, u32[]{:S(2)}) collective-permute-start(bf16[2,1,256]{2,0,1:T(2,128)(2,1)S(1)} %get-tuple-element.49), channel_id=1, source_target_pairs={{16,0},{32,16},{48,32},{64,48},{80,64},{96,80},{112,96},{128,112},... | collective-permute-start | bytes 3080 | tf_op jit(solution)/shard_map/ppermute | solution.py:23
  115.0 11.3 %collective-permute-start.3 = (bf16[2,130,1]{2,0,1:T(2,128)(2,1)S(1)}, bf16[2,130,1]{2,0,1:T(2,128)(2,1)S(1)}, u32[]{:S(2)}, u32[]{:S(2)}) collective-permute-start(bf16[2,130,1]{2,0,1:T(2,128)(2,1)S(1)} %get-tuple-element.50), channel_id=1, source_target_pairs={{1,0},{2,1},{3,2},{4,3},{5,4},{6,5},{7,6},{8,7},{9,8},{10,9},{11,1... | collective-permute-start | bytes 1568 | tf_op jit(solution)/shard_map/ppermute | solution.py:23
  122.8 12.2 %collective-permute-start.2 = (bf16[2,130,1]{2,0,1:T(2,128)(2,1)S(1)}, bf16[2,130,1]{2,0,1:T(2,128)(2,1)S(1)}, u32[]{:S(2)}, u32[]{:S(2)}) collective-permute-start(bf16[2,130,1]{2,0,1:T(2,128)(2,1)S(1)} %get-tuple-element.51), channel_id=1, source_target_pairs={{0,1},{1,2},{2,3},{3,4},{4,5},{5,6},{6,7},{7,8},{8,9},{9,10},{10,1... | collective-permute-start | bytes 1568 | tf_op jit(solution)/shard_map/ppermute | solution.py:22
  150.6 17.1 %copy-start.15 = (bf16[3,3,32,32]{3,2,1,0:T(8,128)(2,1)S(1)}, bf16[3,3,32,32]{3,2,1,0:T(8,128)(2,1)}, u32[]{:S(2)}) copy-start(bf16[3,3,32,32]{3,2,1,0:T(8,128)(2,1)} %param.26) | copy-start | bytes 55300
  159.2 11.1 %collective-permute-start.4 = (bf16[32,1,256]{2,0,1:T(8,128)(2,1)S(1)}, bf16[32,1,256]{2,0,1:T(8,128)(2,1)S(1)}, u32[]{:S(2)}, u32[]{:S(2)}) collective-permute-start(bf16[32,1,256]{2,0,1:T(8,128)(2,1)S(1)} %get-tuple-element.30), channel_id=1, source_target_pairs={{0,16},{16,32},{32,48},{48,64},{64,80},{80,96},{96,112},{112,128},... | collective-permute-start | bytes 49160 | tf_op jit(solution)/shard_map/ppermute | solution.py:22
  161.2 9.2 %collective-permute-start.5 = (bf16[32,1,256]{2,0,1:T(8,128)(2,1)S(1)}, bf16[32,1,256]{2,0,1:T(8,128)(2,1)S(1)}, u32[]{:S(2)}, u32[]{:S(2)}) collective-permute-start(bf16[32,1,256]{2,0,1:T(8,128)(2,1)S(1)} %get-tuple-element.31), channel_id=1, source_target_pairs={{16,0},{32,16},{48,32},{64,48},{80,64},{96,80},{112,96},{128,112},... | collective-permute-start | bytes 49160 | tf_op jit(solution)/shard_map/ppermute | solution.py:23
  176.1 15.4 %collective-permute-start.7 = (bf16[32,130,1]{1,0,2:T(8,128)(2,1)S(1)}, bf16[32,130,1]{1,0,2:T(8,128)(2,1)S(1)}, u32[]{:S(2)}, u32[]{:S(2)}) collective-permute-start(bf16[32,130,1]{1,0,2:T(8,128)(2,1)S(1)} %copy.181), channel_id=1, source_target_pairs={{1,0},{2,1},{3,2},{4,3},{5,4},{6,5},{7,6},{8,7},{9,8},{10,9},{11,1... | collective-permute-start | bytes 24968 | tf_op jit(solution)/shard_map/ppermute | solution.py:23
  178.0 11.6 %collective-permute-start.6 = (bf16[32,130,1]{1,0,2:T(8,128)(2,1)S(1)}, bf16[32,130,1]{1,0,2:T(8,128)(2,1)S(1)}, u32[]{:S(2)}, u32[]{:S(2)}) collective-permute-start(bf16[32,130,1]{1,0,2:T(8,128)(2,1)S(1)} %copy.179), channel_id=1, source_target_pairs={{0,1},{1,2},{2,3},{3,4},{4,5},{5,6},{6,7},{7,8},{8,9},{9,10},{10,1... | collective-permute-start | bytes 24968 | tf_op jit(solution)/shard_map/ppermute | solution.py:22
  224.3 76.7 %copy-start.2 = (bf16[32,128,256]{2,0,1:T(8,128)(2,1)}, bf16[32,128,256]{2,0,1:T(8,128)(2,1)S(1)}, u32[]{:S(2)}) copy-start(bf16[32,128,256]{2,0,1:T(8,128)(2,1)S(1)} %fusion.62) | copy-start | bytes 6291460
  270.5 71.2 %copy-start.14 = (bf16[3,3,64,32]{2,3,1,0:T(8,128)(2,1)S(1)}, bf16[3,3,64,32]{2,3,1,0:T(8,128)(2,1)}, u32[]{:S(2)}) copy-start(bf16[3,3,64,32]{2,3,1,0:T(8,128)(2,1)} %param.28) | copy-start | bytes 110596
  333.0 10.5 %collective-permute-start.8 = (bf16[32,1,128]{2,0,1:T(8,128)(2,1)S(1)}, bf16[32,1,128]{2,0,1:T(8,128)(2,1)S(1)}, u32[]{:S(2)}, u32[]{:S(2)}) collective-permute-start(bf16[32,1,128]{2,0,1:T(8,128)(2,1)S(1)} %get-tuple-element.44), channel_id=1, source_target_pairs={{0,16},{16,32},{32,48},{48,64},{64,80},{80,96},{96,112},{112,128},... | collective-permute-start | bytes 24584 | tf_op jit(solution)/shard_map/ppermute | solution.py:22
  334.9 8.6 %collective-permute-start.9 = (bf16[32,1,128]{2,0,1:T(8,128)(2,1)S(1)}, bf16[32,1,128]{2,0,1:T(8,128)(2,1)S(1)}, u32[]{:S(2)}, u32[]{:S(2)}) collective-permute-start(bf16[32,1,128]{2,0,1:T(8,128)(2,1)S(1)} %get-tuple-element.45), channel_id=1, source_target_pairs={{16,0},{32,16},{48,32},{64,48},{80,64},{96,80},{112,96},{128,112},... | collective-permute-start | bytes 24584 | tf_op jit(solution)/shard_map/ppermute | solution.py:23
  345.1 16.5 %collective-permute-start.10 = (bf16[32,66,1]{1,0,2:T(8,128)(2,1)S(1)}, bf16[32,66,1]{1,0,2:T(8,128)(2,1)S(1)}, u32[]{:S(2)}, u32[]{:S(2)}) collective-permute-start(bf16[32,66,1]{1,0,2:T(8,128)(2,1)S(1)} %copy.183), channel_id=1, source_target_pairs={{0,1},{1,2},{2,3},{3,4},{4,5},{5,6},{6,7},{7,8},{8,9},{9,10},{10,1... | collective-permute-start | bytes 12680 | tf_op jit(solution)/shard_map/ppermute | solution.py:22
  347.1 13.6 %collective-permute-start.11 = (bf16[32,66,1]{1,0,2:T(8,128)(2,1)S(1)}, bf16[32,66,1]{1,0,2:T(8,128)(2,1)S(1)}, u32[]{:S(2)}, u32[]{:S(2)}) collective-permute-start(bf16[32,66,1]{1,0,2:T(8,128)(2,1)S(1)} %copy.185), channel_id=1, source_target_pairs={{1,0},{2,1},{3,2},{4,3},{5,4},{6,5},{7,6},{8,7},{9,8},{10,9},{11,1... | collective-permute-start | bytes 12680 | tf_op jit(solution)/shard_map/ppermute | solution.py:23
  368.8 10.1 %collective-permute-start.12 = (bf16[64,1,128]{2,0,1:T(8,128)(2,1)S(1)}, bf16[64,1,128]{2,0,1:T(8,128)(2,1)S(1)}, u32[]{:S(2)}, u32[]{:S(2)}) collective-permute-start(bf16[64,1,128]{2,0,1:T(8,128)(2,1)S(1)} %get-tuple-element.36), channel_id=1, source_target_pairs={{0,16},{16,32},{32,48},{48,64},{64,80},{80,96},{96,112},{112,128},... | collective-permute-start | bytes 49160 | tf_op jit(solution)/shard_map/ppermute | solution.py:22
  370.8 8.1 %collective-permute-start.13 = (bf16[64,1,128]{2,0,1:T(8,128)(2,1)S(1)}, bf16[64,1,128]{2,0,1:T(8,128)(2,1)S(1)}, u32[]{:S(2)}, u32[]{:S(2)}) collective-permute-start(bf16[64,1,128]{2,0,1:T(8,128)(2,1)S(1)} %get-tuple-element.37), channel_id=1, source_target_pairs={{16,0},{32,16},{48,32},{64,48},{80,64},{96,80},{112,96},{128,112},... | collective-permute-start | bytes 49160 | tf_op jit(solution)/shard_map/ppermute | solution.py:23
  384.4 21.4 %collective-permute-start.15 = (bf16[64,66,1]{1,0,2:T(8,128)(2,1)S(1)}, bf16[64,66,1]{1,0,2:T(8,128)(2,1)S(1)}, u32[]{:S(2)}, u32[]{:S(2)}) collective-permute-start(bf16[64,66,1]{1,0,2:T(8,128)(2,1)S(1)} %copy.189), channel_id=1, source_target_pairs={{1,0},{2,1},{3,2},{4,3},{5,4},{6,5},{7,6},{8,7},{9,8},{10,9},{11,1... | collective-permute-start | bytes 25352 | tf_op jit(solution)/shard_map/ppermute | solution.py:23
  392.2 11.6 %collective-permute-start.14 = (bf16[64,66,1]{1,0,2:T(8,128)(2,1)S(1)}, bf16[64,66,1]{1,0,2:T(8,128)(2,1)S(1)}, u32[]{:S(2)}, u32[]{:S(2)}) collective-permute-start(bf16[64,66,1]{1,0,2:T(8,128)(2,1)S(1)} %copy.187), channel_id=1, source_target_pairs={{0,1},{1,2},{2,3},{3,4},{4,5},{5,6},{6,7},{7,8},{8,9},{9,10},{10,1... | collective-permute-start | bytes 25352 | tf_op jit(solution)/shard_map/ppermute | solution.py:22
  441.9 12.2 %copy-start.16 = (bf16[3,3,32,32]{3,2,1,0:T(8,128)(2,1)S(1)}, bf16[3,3,32,32]{3,2,1,0:T(8,128)(2,1)}, u32[]{:S(2)}) copy-start(bf16[3,3,32,32]{3,2,1,0:T(8,128)(2,1)} %param.35) | copy-start | bytes 55300
  445.5 11.4 %collective-permute-start.16 = (bf16[32,1,256]{2,0,1:T(8,128)(2,1)S(1)}, bf16[32,1,256]{2,0,1:T(8,128)(2,1)S(1)}, u32[]{:S(2)}, u32[]{:S(2)}) collective-permute-start(bf16[32,1,256]{2,0,1:T(8,128)(2,1)S(1)} %get-tuple-element.28), channel_id=1, source_target_pairs={{0,16},{16,32},{32,48},{48,64},{64,80},{80,96},{96,112},{112,128},... | collective-permute-start | bytes 49160 | tf_op jit(solution)/shard_map/ppermute | solution.py:22
  447.4 9.4 %collective-permute-start.17 = (bf16[32,1,256]{2,0,1:T(8,128)(2,1)S(1)}, bf16[32,1,256]{2,0,1:T(8,128)(2,1)S(1)}, u32[]{:S(2)}, u32[]{:S(2)}) collective-permute-start(bf16[32,1,256]{2,0,1:T(8,128)(2,1)S(1)} %get-tuple-element.29), channel_id=1, source_target_pairs={{16,0},{32,16},{48,32},{64,48},{80,64},{96,80},{112,96},{128,112},... | collective-permute-start | bytes 49160 | tf_op jit(solution)/shard_map/ppermute | solution.py:23
  462.5 17.5 %collective-permute-start.19 = (bf16[32,130,1]{1,0,2:T(8,128)(2,1)S(1)}, bf16[32,130,1]{1,0,2:T(8,128)(2,1)S(1)}, u32[]{:S(2)}, u32[]{:S(2)}) collective-permute-start(bf16[32,130,1]{1,0,2:T(8,128)(2,1)S(1)} %copy.195), channel_id=1, source_target_pairs={{1,0},{2,1},{3,2},{4,3},{5,4},{6,5},{7,6},{8,7},{9,8},{10,9},{11,1... | collective-permute-start | bytes 24968 | tf_op jit(solution)/shard_map/ppermute | solution.py:23
  466.6 11.6 %collective-permute-start.18 = (bf16[32,130,1]{1,0,2:T(8,128)(2,1)S(1)}, bf16[32,130,1]{1,0,2:T(8,128)(2,1)S(1)}, u32[]{:S(2)}, u32[]{:S(2)}) collective-permute-start(bf16[32,130,1]{1,0,2:T(8,128)(2,1)S(1)} %copy.193), channel_id=1, source_target_pairs={{0,1},{1,2},{2,3},{3,4},{4,5},{5,6},{6,7},{7,8},{8,9},{9,10},{10,1... | collective-permute-start | bytes 24968 | tf_op jit(solution)/shard_map/ppermute | solution.py:22
  512.9 9.5 %collective-permute-start.20 = (bf16[32,1,256]{2,0,1:T(8,128)(2,1)S(1)}, bf16[32,1,256]{2,0,1:T(8,128)(2,1)S(1)}, u32[]{:S(2)}, u32[]{:S(2)}) collective-permute-start(bf16[32,1,256]{2,0,1:T(8,128)(2,1)S(1)} %get-tuple-element.26), channel_id=1, source_target_pairs={{0,16},{16,32},{32,48},{48,64},{64,80},{80,96},{96,112},{112,128},... | collective-permute-start | bytes 49160 | tf_op jit(solution)/shard_map/ppermute | solution.py:22
  514.8 7.8 %collective-permute-start.21 = (bf16[32,1,256]{2,0,1:T(8,128)(2,1)S(1)}, bf16[32,1,256]{2,0,1:T(8,128)(2,1)S(1)}, u32[]{:S(2)}, u32[]{:S(2)}) collective-permute-start(bf16[32,1,256]{2,0,1:T(8,128)(2,1)S(1)} %get-tuple-element.27), channel_id=1, source_target_pairs={{16,0},{32,16},{48,32},{64,48},{80,64},{96,80},{112,96},{128,112},... | collective-permute-start | bytes 49160 | tf_op jit(solution)/shard_map/ppermute | solution.py:23
  529.5 20.4 %collective-permute-start.23 = (bf16[32,130,1]{1,0,2:T(8,128)(2,1)}, bf16[32,130,1]{1,0,2:T(8,128)(2,1)}, u32[]{:S(2)}, u32[]{:S(2)}) collective-permute-start(bf16[32,130,1]{1,0,2:T(8,128)(2,1)} %copy.199), channel_id=1, source_target_pairs={{1,0},{2,1},{3,2},{4,3},{5,4},{6,5},{7,6},{8,7},{9,8},{10,9},{11,1... | collective-permute-start | bytes 24968 | tf_op jit(solution)/shard_map/ppermute | solution.py:23
  535.3 12.0 %collective-permute-start.22 = (bf16[32,130,1]{1,0,2:T(8,128)(2,1)}, bf16[32,130,1]{1,0,2:T(8,128)(2,1)}, u32[]{:S(2)}, u32[]{:S(2)}) collective-permute-start(bf16[32,130,1]{1,0,2:T(8,128)(2,1)} %copy.197), channel_id=1, source_target_pairs={{0,1},{1,2},{2,3},{3,4},{4,5},{5,6},{6,7},{7,8},{8,9},{9,10},{10,1... | collective-permute-start | bytes 24968 | tf_op jit(solution)/shard_map/ppermute | solution.py:22
  (26 other events, 101.2 us)
where the time goes:
time: 573 us; the launch traced here: 563 us
  local copies, waits for them, and re-layouts  183 us (32%)
  matrix products  146 us (25%)
  starting transfers between devices  132 us (23%)
  waiting for transfers between devices  54.7 us (10%)
  other arithmetic  26.5 us (5%)
  blocking collectives  18.5 us (3%)
    dot_general x53, matrix products, conv_valid(): jnp.einsum('oc,chw->ohw', weight[row_shift, col_shift], window, preferred...  125 us
    ppermute x12, starting transfers between devices, padded_2(): after = lax.ppermute(initial, axis, down)  76.5 us
    slice x1, local copies, waits for them, and re-layouts, shards(): encoded[:, 1::2, 0::2].astype(jnp.float32)  30.5 us
    slice x1, local copies, waits for them, and re-layouts, shards(): encoded[:, 0::2, 0::2].astype(jnp.float32)  30.5 us
    ppermute x12, waiting for transfers between devices, padded_2(): before = lax.ppermute(last, axis, up)  28.3 us
    ppermute x12, starting transfers between devices, padded_2(): before = lax.ppermute(last, axis, up)  25.2 us
    slice x1, local copies, waits for them, and re-layouts, shards(): encoded[:, 1::2, 1::2].astype(jnp.float32)  23.4 us
    slice x1, local copies, waits for them, and re-layouts, shards(): encoded[:, 0::2, 1::2].astype(jnp.float32)  22.7 us
  transfers between devices with their start and end apart: 27, of which 9 were waited for; matrix products, arithmetic and copies ran while one was open for 8% of the time, Pallas kernels for 0%

commit v1 on v0

v1 whole, which is shorter than its diff:
```python
import functools
import math

import jax
import jax.numpy as jnp
import numpy as np
from jax import lax
from jax.experimental import pallas as pl
from jax.experimental.pallas import tpu as pltpu
from jax.sharding import PartitionSpec as P

MESH = pl.DeviceIdType.MESH
F32 = jnp.float32
BF16 = jnp.bfloat16

NX, NY = 32, 16
SLABS = 18
STRIPES = 16
PIX = SLABS * STRIPES
PIX2 = PIX // 2
GROUPS = 18


def dot(a, b):
    return jnp.dot(a, b, preferred_element_type=F32)


def dot_nt(a, b):
    return lax.dot_general(a, b, (((1,), (1,)), ((), ())), preferred_element_type=F32)


def complex_block(c, s):
    return np.stack([np.stack([c, -s]), np.stack([s, c])])


def transform_constants():
    turn = 2.0 * math.pi
    y0 = np.arange(128)
    cells = np.arange(256)
    ang = turn * (np.outer(y0, y0) % 128) / 128
    first = complex_block(np.cos(ang), np.sin(ang))
    first = first.transpose(0, 2, 3, 1).reshape(256, 256)
    ang = turn * np.outer(y0, cells % 32) / 4096
    sign = np.where(y0 % 2 == 0, 1.0, -1.0)[:, None]
    twist1 = np.stack([np.cos(ang) * sign, np.sin(ang) * sign])
    short = np.arange(32)
    ang = turn * (np.outer(short, short) % 32) / 32
    c32, s32 = np.cos(ang), np.sin(ang)
    second = complex_block(c32, s32)
    second = np.einsum("abys,rt->yarbts", second, np.eye(8)).reshape(512, 512)
    third = complex_block(c32, s32)
    third = np.einsum("abxi,yz->ayxibz", third, np.eye(8)).reshape(512, 512)
    ang = turn * np.outer(y0, y0) / 4096
    twist2 = np.stack([np.cos(ang) * sign, np.sin(ang) * sign]) / 4096
    ang = turn * (np.outer(short, y0) % 32) / 32
    fourth = np.concatenate([np.cos(ang), -np.sin(ang)], axis=1)
    return (
        jnp.asarray(first, BF16),
        jnp.asarray(twist1, F32),
        jnp.asarray(second, BF16),
        jnp.asarray(third, BF16),
        jnp.asarray(twist2, F32),
        jnp.asarray(fourth, BF16),
        jnp.asarray(np.eye(128), BF16),
    )


def permutations():
    into = np.zeros((20, STRIPES, 384), np.float32)
    back = np.zeros((256, SLABS, STRIPES), np.float32)
    for w in range(-1, SLABS + 1):
        for s in range(STRIPES):
            col = SLABS * s + w - 8
            if 0 <= col < 264:
                into[w + 1, s, col] = 1
            elif -8 <= col < 0:
                into[w + 1, s, 384 + col] = 1
            if 0 <= col < 256 and 0 <= w < SLABS:
                back[col, w, s] = 1
    return jnp.asarray(into.reshape(320, 384), BF16), jnp.asarray(back.reshape(256, PIX), BF16)


def send_all(axis, count, me, source, landing, send_sem, recv_sem):
    def one(step, carry):
        other = lax.rem(me + step, count)
        pltpu.make_async_remote_copy(
            src_ref=source.at[other],
            dst_ref=landing.at[me],
            send_sem=send_sem,
            recv_sem=recv_sem,
            device_id={axis: other},
            device_id_type=MESH,
        ).start()
        return carry

    lax.fori_loop(1, count, one, 0)
    landing[me] = source[me]


def wait_bytes(ref, sem):
    pltpu.make_async_copy(ref, ref, sem).wait()


def grid_tiles(vis, owner, kernels):
    rows = lax.broadcasted_iota(jnp.int32, (256, 512), 0)
    tiles = rows // 2
    real = (rows % 2) == 0
    total = None
    for piece in range(8):
        lanes = slice(512 * piece, 512 * piece + 512)
        both = jnp.where(real, vis[0:1, lanes].astype(F32), vis[1:2, lanes].astype(F32))
        chosen = jnp.where(owner[0:1, lanes] == tiles, both, 0.0).astype(BF16)
        term = dot(chosen, kernels[lanes, :])
        total = term if total is None else total + term
    return total


def column_transform(held, first, twist1, second):
    turned = dot(first[...], held)
    real, imag = turned[:128], turned[128:]
    c, s = twist1[0], twist1[1]
    both = jnp.concatenate([real * c - imag * s, real * s + imag * c], axis=1).astype(BF16)
    return dot_nt(second[...], both)


def columns_up(held, eye):
    wide = held.astype(F32).reshape(16, 4, 8, 128)
    halves = []
    for y1 in range(2):
        parts = []
        for part in range(2):
            piece = wide[:, 2 * y1 + part].reshape(128, 128).astype(BF16)
            parts.append(dot_nt(eye, piece).reshape(16, 8, 128))
        halves.append(jnp.concatenate(parts, axis=1))
    return jnp.concatenate(halves, axis=0).astype(BF16)


def row_transform(held, third, twist2, fourth, store):
    turned = dot(third[...], held)
    for y in range(8):
        real = turned[32 * y : 32 * y + 32]
        imag = turned[256 + 32 * y : 256 + 32 * y + 32]
        real = jnp.concatenate([real] * 4, axis=0)
        imag = jnp.concatenate([imag] * 4, axis=0)
        c, s = twist2[0], twist2[1]
        both = jnp.concatenate([real * c - imag * s, real * s + imag * c], axis=1).astype(BF16)
        store(y, dot_nt(fourth[...], both))


def exchange_kernel(
    vis,
    owner,
    kernels,
    sky,
    first,
    twist1,
    second,
    third,
    twist2,
    fourth,
    eye,
    dirty_out,
    rows_out,
    cols_out,
    tiles,
    landed1,
    bands,
    landed2,
    ups,
    landed3,
    image,
    downs,
    landed4,
    sides,
    sky_rows,
    sky_sides,
    sky_cols,
    sky_own,
    send_sem,
    recv_sem,
):
    gx, gy = lax.axis_index("gx"), lax.axis_index("gy")
    barrier = pltpu.get_barrier_semaphore()

    def greet(axis, count, me):
        def one(step, carry):
            pl.semaphore_signal(
                barrier, inc=1, device_id={axis: lax.rem(me + step, count)}, device_id_type=MESH
            )
            return carry

        lax.fori_loop(1, count, one, 0)

    greet("gy", NY, gy)
    greet("gx", NX, gx)

    sky_own[...] = sky[...].astype(BF16)
    summed = grid_tiles(vis, owner, kernels)
    tiles[...] = summed.astype(BF16).reshape(16, 16, 256)
    pl.semaphore_wait(barrier, NX + NY - 2)

    send_all("gy", NY, gy, tiles, landed1, send_sem.at[0], recv_sem.at[0])

    def to_side(source, target, slot, axis, other):
        return pltpu.make_async_remote_copy(
            src_ref=source,
            dst_ref=target,
            send_sem=send_sem.at[slot],
            recv_sem=recv_sem.at[slot],
            device_id={axis: other},
            device_id_type=MESH,
        )

    down_x, up_x = lax.rem(gx + 1, NX), lax.rem(gx + NX - 1, NX)
    right_y, left_y = lax.rem(gy + 1, NY), lax.rem(gy + NY - 1, NY)
    row_copies = [
        to_side(sky_own.at[pl.ds(112, 16)], sky_rows.at[0], 4, "gx", down_x),
        to_side(sky_own.at[pl.ds(0, 16)], sky_rows.at[1], 5, "gx", up_x),
    ]
    for copy in row_copies:
        copy.start()

    wait_bytes(landed1.at[pl.ds(0, 15)], recv_sem.at[0])
    turned = column_transform(landed1[...].reshape(256, 256), first, twist1, second)
    bands[...] = turned.astype(BF16).reshape(16, 32, 128)
    send_all("gy", NY, gy, bands, landed2, send_sem.at[1], recv_sem.at[1])

    for copy in row_copies:
        copy.wait()
    for half in range(2):
        lanes = slice(128 * half, 128 * half + 128)
        sky_cols[half, 0:16] = sky_rows[0, :, lanes]
        sky_cols[half, 16:144] = sky_own[:, lanes]
        sky_cols[half, 144:160] = sky_rows[1, :, lanes]
    col_copies = [
        to_side(sky_cols.at[1], sky_sides.at[0], 6, "gy", right_y),
        to_side(sky_cols.at[0], sky_sides.at[1], 7, "gy", left_y),
    ]
    for copy in col_copies:
        copy.start()

    wait_bytes(landed2.at[pl.ds(0, 15)], recv_sem.at[1])
    ups[...] = columns_up(landed2[...], eye[...])
    send_all("gx", NX, gx, ups, landed3, send_sem.at[2], recv_sem.at[2])

    wait_bytes(landed3.at[pl.ds(0, 31)], recv_sem.at[2])

    def store(y, value):
        image[pl.ds(8 + y, 32, stride=8), :] = value

    image[0:8] = jnp.zeros((8, 128), F32)
    image[264:272] = jnp.zeros((8, 128), F32)
    row_transform(landed3[...].reshape(512, 128), third, twist2, fourth, store)
    whole = image[...].reshape(34, 8, 128)
    lane = lax.broadcasted_iota(jnp.int32, (32, 8, 128), 2)
    outer = jnp.where(lane < 64, whole[2:34], whole[0:32])
    downs[...] = jnp.concatenate([whole[1:33], outer], axis=1).astype(BF16)
    send_all("gx", NX, gx, downs, landed4, send_sem.at[3], recv_sem.at[3])

    for copy in col_copies:
        copy.wait()
    rows_out[...] = sky_rows[...]
    cols_out[...] = sky_sides[...]

    wait_bytes(landed4.at[pl.ds(0, 31)], recv_sem.at[3])
    side_copies = [
        to_side(landed4.at[31], sides.at[0], 8, "gy", right_y),
        to_side(landed4.at[0], sides.at[1], 9, "gy", left_y),
    ]
    for copy in side_copies:
        copy.start()
    dirty_out[0:32] = landed4[...]
    for copy in side_copies:
        copy.wait()
    dirty_out[32:34] = sides[...]
    wait_bytes(tiles.at[pl.ds(0, 15)], send_sem.at[0])
    wait_bytes(bands.at[pl.ds(0, 15)], send_sem.at[1])
    wait_bytes(ups.at[pl.ds(0, 31)], send_sem.at[2])
    wait_bytes(downs.at[pl.ds(0, 31)], send_sem.at[3])


def exchange(vis, owner, kernels, sky):
    vmem = pl.BlockSpec(memory_space=pltpu.VMEM)
    constants = transform_constants()
    return pl.pallas_call(
        exchange_kernel,
        out_shape=(
            jax.ShapeDtypeStruct((34, 16, 128), BF16),
            jax.ShapeDtypeStruct((2, 16, 256), BF16),
            jax.ShapeDtypeStruct((2, 160, 128), BF16),
        ),
        in_specs=[vmem] * 11,
        out_specs=(vmem, vmem, vmem),
        scratch_shapes=[
            pltpu.VMEM((16, 16, 256), BF16),
            pltpu.VMEM((16, 16, 256), BF16),
            pltpu.VMEM((16, 32, 128), BF16),
            pltpu.VMEM((16, 32, 128), BF16),
            pltpu.VMEM((32, 16, 128), BF16),
            pltpu.VMEM((32, 16, 128), BF16),
            pltpu.VMEM((272, 128), F32),
            pltpu.VMEM((32, 16, 128), BF16),
            pltpu.VMEM((32, 16, 128), BF16),
            pltpu.VMEM((2, 16, 128), BF16),
            pltpu.VMEM((2, 16, 256), BF16),
            pltpu.VMEM((2, 160, 128), BF16),
            pltpu.VMEM((2, 160, 128), BF16),
            pltpu.VMEM((128, 256), BF16),
            pltpu.SemaphoreType.DMA((10,)),
            pltpu.SemaphoreType.DMA((10,)),
        ],
        compiler_params=pltpu.CompilerParams(
            collective_id=0, has_side_effects=True, vmem_limit_bytes=40 << 20
        ),
        name="exchange",
    )(vis, owner, kernels, sky, *constants)


def band(dst, tiles, taps_high, rows, start, lane_id, count, per_dc):
    for dc in range(3):
        for row in range(rows):
            block = None
            for p in range(3):
                out_row = row - start - p
                if 0 <= out_row < count:
                    term = jnp.where(lane_id == out_row, tiles[3 * p + dc].astype(F32), 0.0)
                    block = term if block is None else block + term
            if block is None:
                block = jnp.zeros(lane_id.shape, F32)
            at = dc * per_dc + row * taps_high
            dst[at : at + taps_high, :] = block.astype(BF16)


def network_kernel(
    sky,
    dirty_in,
    rows_in,
    cols_in,
    into,
    back,
    eye,
    biases,
    enter_t,
    encode_t,
    coarse_t,
    deeper_t,
    decode_t,
    output_t,
    upward_t,
    skip_t,
    dirty_out,
    estimate_out,
    window,
    entry,
    fine_a,
    fine_b,
    fine_c,
    pooled,
    coarse,
    deep,
    mask,
    w_enter,
    w_encode,
    w_coarse,
    w_deeper,
    w_decode,
    w_output,
    w_upward,
    w_skip,
    w_pool,
    drawn,
):
    gx, gy = lax.axis_index("gx"), lax.axis_index("gy")
    last_x, last_y = lax.axis_size("gx") - 1, lax.axis_size("gy") - 1
    keep_top = jnp.where(gx == 0, 0.0, 1.0).astype(F32)
    keep_bottom = jnp.where(gx == last_x, 0.0, 1.0).astype(F32)

    lane32 = lax.broadcasted_iota(jnp.int32, (32, 256), 1)
    band(w_encode, encode_t, 32, 16, 3, lane32 // 32, 8, 512)
    band(w_decode, decode_t, 32, 16, 3, lane32 // 32, 8, 512)
    band(w_coarse, coarse_t, 32, 12, 3, lane32 // 64, 4, 384)
    lane64 = lax.broadcasted_iota(jnp.int32, (64, 256), 1)
    band(w_deeper, deeper_t, 64, 8, 1, lane64 // 64, 4, 512)
    lane_out = lax.broadcasted_iota(jnp.int32, (32, 128), 1)
    band(w_output, output_t, 32, 16, 3, lane_out % 8, 8, 512)
    for row in range(4):
        term = jnp.where(lane64 // 64 == row, upward_t[...].astype(F32), 0.0)
        w_upward[64 * row : 64 * row + 64, :] = term.astype(BF16)
    for row in range(8):
        term = jnp.where(lane32 // 32 == row, skip_t[...].astype(F32), 0.0)
        w_skip[32 * row : 32 * row + 32, :] = term.astype(BF16)
    rows512 = lax.broadcasted_iota(jnp.int32, (512, 128), 0)
    lanes512 = lax.broadcasted_iota(jnp.int32, (512, 128), 1)
    pairs = ((rows512 % 256) // 64 == lanes512 // 32) & (rows512 % 32 == lanes512 % 32)
    w_pool[...] = jnp.where(pairs, 0.25, 0.0).astype(BF16)
    row_id = lax.broadcasted_iota(jnp.int32, (64, 256), 0)
    for variant in range(4):
        for dc in range(3):
            for channel in range(2):
                block = jnp.zeros((64, 256), F32)
                for p in range(3):
                    tap = 6 * p + 2 * dc + channel
                    hit = row_id - 15 - 8 * variant - p == lane64 // 32
                    block = block + jnp.where(hit, enter_t[tap : tap + 1, :].astype(F32), 0.0)
                at = dc * 128 + channel * 64
                w_enter[variant, at : at + 64, :] = block.astype(BF16)

    slab = lax.broadcasted_iota(jnp.int32, (20, 16, 128), 0)
    stripe = lax.broadcasted_iota(jnp.int32, (20, 16, 128), 1)
    col = SLABS * stripe + slab - 9 + 256 * gy
    mask[...] = jnp.where((col >= 0) & (col < 256 * (last_y + 1)), 1.0, 0.0).astype(F32)

    lane = lax.broadcasted_iota(jnp.int32, (160, 128), 1)
    beside = jnp.where(lane < 64, cols_in[1].astype(F32), cols_in[0].astype(F32))
    above = rows_in[0].astype(F32)[8:16] * keep_top
    below = rows_in[1].astype(F32)[0:8] * keep_bottom
    zeros = jnp.zeros((32, 256), F32)
    window[0, :, 0:256] = jnp.concatenate(
        [zeros[:16], above, sky[...], below, zeros], axis=0
    ).astype(BF16)
    beside = jnp.concatenate(
        [
            zeros[:16, :128],
            beside[8:16] * keep_top,
            beside[16:144],
            beside[144:152] * keep_bottom,
            zeros[:, :128],
        ],
        axis=0,
    )
    window[0, :, 256:384] = beside.astype(BF16)
    wide = dirty_in[...].astype(F32)
    gap = jnp.zeros((112, 128), F32)
    parts = []
    for half in range(2):
        rows8 = slice(8 * half, 8 * half + 8)
        stacked = jnp.concatenate(
            [wide[0:32, rows8].reshape(256, 128), wide[33, rows8], gap, wide[32, rows8]], axis=0
        )
        parts.append(dot_nt(eye[...], stacked.astype(BF16)))
    dirty_out[...] = parts[0][:, 0:256]
    zeros = jnp.zeros((32, 384), F32)
    window[1] = jnp.concatenate(
        [zeros[:16], parts[1][120:128] * keep_top, parts[0], parts[1][0:8] * keep_bottom, zeros],
        axis=0,
    ).astype(BF16)
    for q in range(5):
        rows64 = slice(32 * q, 32 * q + 64)
        both = jnp.concatenate([window[0, rows64], window[1, rows64]], axis=0)
        placed = dot_nt(into[...], both).reshape(20, 16, 128) * mask[...]
        entry[q] = placed.astype(BF16)

    blank = jnp.zeros((20, 16, 128), BF16)
    for ref, top in ((fine_a, 37), (fine_b, 37), (fine_c, 37), (pooled, 19), (coarse, 37)):
        ref[0] = blank[: ref.shape[1]]
        ref[top] = blank[: ref.shape[1]]

    def row_keep(group):
        top = jnp.where(group == 0, keep_top, 1.0)
        bottom = jnp.where(group == GROUPS - 1, keep_bottom, 1.0)
        return top * bottom

    def put(ref, at, value, slabs):
        ref[at, 1 : slabs + 1] = value.astype(BF16)
        ref[at, 0] = pltpu.roll(value[slabs - 1], 1, 0).astype(BF16)
        ref[at, slabs + 1] = pltpu.roll(value[0], STRIPES - 1, 0).astype(BF16)

    def finish(total, bias_row, keep):
        value = jnp.maximum(total + biases[bias_row : bias_row + 1, :], 0.0)
        scaled = mask[1:19] * keep
        return [
            value[:, 128 * h : 128 * h + 128].reshape(SLABS, 16, 128) * scaled for h in range(2)
        ]

    def gathered(ref, at, high, slabs):
        pieces = [
            ref[at + h, dc : dc + slabs].reshape(slabs * 16, 128)
            for dc in range(3)
            for h in range(high)
        ]
        return jnp.concatenate(pieces, axis=1)

    def enter_step(group, carry):
        tile, variant = group // 4, group % 4
        pieces = [entry[tile, dc : dc + SLABS].reshape(PIX, 128) for dc in range(3)]
        total = dot(jnp.concatenate(pieces, axis=1), w_enter[variant])
        for h, value in enumerate(finish(total, 0, row_keep(group))):
            put(fine_a, 2 * group + 1 + h, value, SLABS)
        return carry

    lax.fori_loop(0, GROUPS, enter_step, 0)

    def encode_step(group, carry):
        total = dot(gathered(fine_a, 2 * group, 4, SLABS), w_encode[...])
        halves = finish(total, 1, row_keep(group))
        evens, odds = [], []
        for h, value in enumerate(halves):
            put(fine_b, 2 * group + 1 + h, value, SLABS)
            split = value.reshape(SLABS // 2, 2, 16, 128)
            evens.append(split[:, 0].reshape(PIX2, 128))
            odds.append(split[:, 1].reshape(PIX2, 128))
        small = dot(jnp.concatenate(evens + odds, axis=1).astype(BF16), w_pool[...])
        put(pooled, group + 1, small.reshape(SLABS // 2, 16, 128), SLABS // 2)
        return carry

    lax.fori_loop(0, GROUPS, encode_step, 0)

    def coarse_mask(keep):
        even = mask[1:19].reshape(SLABS // 2, 2, 16, 128)[:, 0]
        return even * keep

    def coarse_step(group, carry):
        total = dot(gathered(pooled, group, 3, SLABS // 2), w_coarse[...])
        value = jnp.maximum(total + biases[2:3, :], 0.0)
        scaled = coarse_mask(row_keep(group))
        for h in range(2):
            half = value[:, 128 * h : 128 * h + 128].reshape(SLABS // 2, 16, 128) * scaled
            put(coarse, 2 * group + 1 + h, half, SLABS // 2)
        return carry

    lax.fori_loop(0, GROUPS, coarse_step, 0)

    def merge_step(group, carry):
        total = dot(gathered(coarse, 2 * group, 4, SLABS // 2), w_deeper[...])
        value = jnp.maximum(total + biases[3:4, :], 0.0).astype(BF16)
        lifted = dot(value, w_upward[...]).reshape(SLABS // 2, 1, 16, 256)
        own = jnp.concatenate(
            [fine_b[2 * group + 1 + h, 1:19].reshape(PIX, 128) for h in range(2)], axis=1
        )
        skipped = dot(own, w_skip[...]).reshape(SLABS // 2, 2, 16, 256)
        total = (skipped + lifted).reshape(PIX, 256)
        for h, half in enumerate(finish(total, 4, row_keep(group))):
            put(fine_a, 2 * group + 1 + h, half, SLABS)
        return carry

    lax.fori_loop(0, GROUPS, merge_step, 0)

    def decode_step(group, carry):
        total = dot(gathered(fine_a, 2 * group, 4, SLABS), w_decode[...])
        for h, half in enumerate(finish(total, 5, row_keep(group))):
            put(fine_c, 2 * group + 1 + h, half, SLABS)
        return carry

    lax.fori_loop(0, GROUPS, decode_step, 0)

    lane_row = lax.broadcasted_iota(jnp.int32, (PIX, 128), 1) // 8

    def output_step(group, carry):
        total = dot(gathered(fine_c, 2 * group, 4, SLABS), w_output[...])
        drawn[...] = jnp.where(lane_row == group - 1, total, drawn[...])
        return carry

    drawn[...] = jnp.zeros((PIX, 128), F32)
    lax.fori_loop(1, GROUPS - 1, output_step, 0)

    update = drawn[...]
    high = update.astype(BF16)
    low = (update - high.astype(F32)).astype(BF16)
    ordered = dot(back[...], high) + dot(back[...], low)
    estimate_out[...] = sky[...] + ordered.T


def network(sky, dirty_in, rows_in, cols_in, weights):
    vmem = pl.BlockSpec(memory_space=pltpu.VMEM)
    into, back = permutations()
    eye = jnp.asarray(np.eye(128), BF16)
    operands = (sky, dirty_in, rows_in, cols_in, into, back, eye) + weights
    return pl.pallas_call(
        network_kernel,
        out_shape=(
            jax.ShapeDtypeStruct((128, 256), F32),
            jax.ShapeDtypeStruct((128, 256), F32),
        ),
        in_specs=[vmem] * len(operands),
        out_specs=(vmem, vmem),
        scratch_shapes=[
            pltpu.VMEM((2, 192, 384), BF16),
            pltpu.VMEM((5, 20, 16, 128), BF16),
            pltpu.VMEM((38, 20, 16, 128), BF16),
            pltpu.VMEM((38, 20, 16, 128), BF16),
            pltpu.VMEM((38, 20, 16, 128), BF16),
            pltpu.VMEM((20, 11, 16, 128), BF16),
            pltpu.VMEM((38, 11, 16, 128), BF16),
            pltpu.VMEM((8, 128), BF16),
            pltpu.VMEM((20, 16, 128), F32),
            pltpu.VMEM((4, 384, 256), BF16),
            pltpu.VMEM((1536, 256), BF16),
            pltpu.VMEM((1152, 256), BF16),
            pltpu.VMEM((1536, 256), BF16),
            pltpu.VMEM((1536, 256), BF16),
            pltpu.VMEM((1536, 128), BF16),
            pltpu.VMEM((256, 256), BF16),
            pltpu.VMEM((256, 256), BF16),
            pltpu.VMEM((512, 128), BF16),
            pltpu.VMEM((PIX, 128), F32),
        ],
        compiler_params=pltpu.CompilerParams(vmem_limit_bytes=48 << 20),
        name="network",
    )(*operands)


def tap_tiles(weight, copies):
    turned = jnp.swapaxes(weight, 2, 3)
    turned = jnp.tile(turned, (1, 1, 1, copies))
    return turned.reshape(9, turned.shape[2], turned.shape[3])


def network_weights(ew, eb, nw, nb, cw, cb, dw, db, uw, sw, mb, ow, ob, fw):
    biases = jnp.stack(
        [
            jnp.tile(eb, 8),
            jnp.tile(nb, 8),
            jnp.tile(cb, 4),
            jnp.tile(db, 4),
            jnp.tile(mb, 8),
            jnp.tile(ob, 8),
            jnp.zeros((256,), F32),
            jnp.zeros((256,), F32),
        ]
    )
    enter = jnp.tile(jnp.swapaxes(ew, 2, 3).reshape(18, 32), (1, 8))
    return (
        biases,
        enter,
        tap_tiles(nw, 8),
        tap_tiles(cw, 4),
        tap_tiles(dw, 4),
        tap_tiles(ow, 8),
        tap_tiles(fw, 128),
        jnp.tile(uw.T, (1, 8)),
        jnp.tile(sw.T, (1, 8)),
    )


def shards(
    sky_image,
    visibilities,
    grid_kernels,
    tile_counts,
    block_tiles,
    *parameters,
):
    slots = block_tiles.shape[2]
    live = jnp.arange(slots, dtype=jnp.int32) < jnp.sum(tile_counts[0, 0])
    owner = jnp.repeat(jnp.where(live, block_tiles[0, 0], -1), 64).reshape(1, slots * 64)
    vis = jnp.swapaxes(visibilities[0, 0], 0, 1).reshape(2, slots * 64)
    kernels = grid_kernels.reshape(slots * 64, 256)
    dirty, rows, cols = exchange(vis, owner, kernels, sky_image)
    return network(sky_image, dirty, rows, cols, network_weights(*parameters))


def solution(mesh):
    block = P("gx", "gy")
    return jax.shard_map(
        shards,
        mesh=mesh,
        in_specs=(
            block,
            P("gx", "gy", None, None, None),
            P("gx", "gy", None, None, None),
            P("gx", "gy", None),
            P("gx", "gy", None),
        )
        + (P(),) * 14,
        out_specs=(block, block),
        check_vma=False,
    )
```

time: 573 us -> 121 us (0.21)
  the two profiles are of different devices: /device:TPU:130 before, /device:TPU:1 now
where the time goes in v1:
time: 121 us
  Pallas kernels  104 us (86%)
  local copies, waits for them, and re-layouts  13.2 us (11%)
  other arithmetic  2.63 us (2%)
    pallas_call x1, Pallas kernels, exchange(): pl.pallas_call(exchange_kernel, out_shape=(jax.ShapeDtypeStruct((34, 16,...  57.7 us
    pallas_call x1, Pallas kernels, network(): pl.pallas_call(network_kernel, out_shape=(jax.ShapeDtypeStruct((128, 256)...  46.2 us
    unnamed x54, local copies, waits for them, and re-layouts  8.91 us

profile of v1, /device:TPU:1, one launch (start us, length us, event | category | flops | bytes accessed | tf_op | source)
XLA Modules:
  0.0 120.7 jit_solution(17527226999309154718)
XLA Ops:
  0.6 1.3 %reduce_sum.9 = s32[]{:T(128)} reduce(s32[1,1,128]{2,1,0:T(1,128)} %param.32, s32[]{:T(128)} %constant.9.clone.1), dimensions={0,1,2}, to_apply=%region_0.0 | reduce | flops 127 | bytes 520 | tf_op jit(solution)/shard_map/reduce_sum | solution.py:644
  2.0 1.3 %compare_select_fusion = s32[64]{0:T(128)S(1)} fusion(s32[1,1,64]{2,1,0:T(1,128)} %param.33, s32[]{:T(128)} %reduce_sum.9), kind=kLoop, calls=%fused_computation | loop fusion | flops 128 | bytes 516 | tf_op jit(solution)/shard_map/jit(_where)/select_n | solution.py:645
  3.3 0.1 reshape_reshape.3.owner
  3.4 0.8 copy.37
  4.2 0.1 reshape.51.vis
  4.3 1.6 %copy-done = bf16[1,1,64,64,256]{4,3,2,1,0:T(8,128)(2,1)S(1)} copy-done((bf16[1,1,64,64,256]{4,3,2,1,0:T(8,128)(2,1)S(1)}, bf16[1,1,64,64,256]{4,3,2,1,0:T(8,128)(2,1)}, u32[]{:S(2)}) %copy-start) | copy-done | bytes 2097176
  5.9 1.0 copy-done.1
  7.0 1.0 copy-done.2
  8.0 0.9 copy-done.3
  8.9 0.9 copy-done.5
  9.8 0.8 copy-done.8
  10.6 0.9 copy-done.10
  11.5 0.9 copy-done.11
  12.4 0.7 copy-done.12
  13.1 57.7 %exchange.1 = (bf16[34,16,128]{2,1,0:T(8,128)(2,1)S(1)}, bf16[2,16,256]{2,1,0:T(8,128)(2,1)S(1)}, bf16[2,160,128]{2,1,0:T(8,128)(2,1)S(1)}) custom-call(bf16[2,4096]{1,0:T(2,128)(2,1)S(1)} %reshape.51.vis, s32[1,4096]{1,0:T(1,128)S(1)} %reshape_reshape.3.owner, bf16[4096,256]{1,0:T(8,128)(2,1)S(1)} %bitcast.28, f32[128,256]{1,0:T(8,128)S(1)} %copy-done.3, ...), custom_call_target="tpu_custom_call" | custom-call | tf_op jit(solution)/shard_map/exchange/pallas_call | solution.py:285
  70.9 0.1 copy.39
  71.0 0.2 tile.116
  71.2 0.4 tile.117.deeper_t
  71.6 0.1 copy.40
  72.0 0.4 tile.119.decode_t
  72.4 0.1 copy.38
  72.5 0.1 tile.55
  72.6 0.4 tile.56.encode_t
  73.1 0.2 tile.115.coarse_t
  73.3 0.1 copy.42.upward_t
  73.4 0.1 copy.41
  73.6 0.1 tile.125.skip_t
  73.7 0.1 tile.121.output_t
  73.8 0.1 tile.54.enter_t
  74.3 0.1 stack_tile.20
  74.4 0.1 stack_tile.21
  74.6 46.2 %network.1 = (f32[128,256]{1,0:T(8,128)}, f32[128,256]{1,0:T(8,128)}) custom-call(f32[128,256]{1,0:T(8,128)S(1)} %copy-done.4, bf16[34,16,128]{2,1,0:T(8,128)(2,1)S(1)} %get-tuple-element.5.dirty_in, bf16[2,16,256]{2,1,0:T(8,128)(2,1)S(1)} %get-tuple-element.6.rows_in, bf16[2,160,128]{2,1,0:T(8,128)(2,1)S(1)} %get-tuple-element.7.cols_in, ...), custom_call_target="tpu_custom_call" | custom-call | tf_op jit(solution)/shard_map/network/pallas_call | solution.py:568
  (65 shorter events, 0.8 us)
Async XLA Ops:
  0.6 70.2 %copy-start.13 = (bf16[3,3,64,64]{3,2,1,0:T(8,128)(2,1)S(1)}, bf16[3,3,64,64]{3,2,1,0:T(8,128)(2,1)}, u32[]{:S(2)}) copy-start(bf16[3,3,64,64]{3,2,1,0:T(8,128)(2,1)} %param.40) | copy-start | bytes 221188
  4.3 1.6 %copy-start = (bf16[1,1,64,64,256]{4,3,2,1,0:T(8,128)(2,1)S(1)}, bf16[1,1,64,64,256]{4,3,2,1,0:T(8,128)(2,1)}, u32[]{:S(2)}) copy-start(bf16[1,1,64,64,256]{4,3,2,1,0:T(8,128)(2,1)} %param.31) | copy-start | bytes 6291460
  5.9 1.0 copy-start.1
  6.9 1.0 copy-start.2
  8.0 0.9 copy-start.3
  8.9 0.9 copy-start.5
  9.8 0.8 copy-start.8
  10.6 0.9 copy-start.10
  11.5 0.9 copy-start.11
  12.4 0.7 copy-start.12
  13.1 58.5 %copy-start.14 = (bf16[3,3,32,32]{3,2,1,0:T(8,128)(2,1)S(1)}, bf16[3,3,32,32]{3,2,1,0:T(8,128)(2,1)}, u32[]{:S(2)}) copy-start(bf16[3,3,32,32]{3,2,1,0:T(8,128)(2,1)} %param.45) | copy-start | bytes 55300
  70.8 1.5 %copy-start.15 = (bf16[3,3,32,32]{3,2,1,0:T(8,128)(2,1)S(1)}, bf16[3,3,32,32]{3,2,1,0:T(8,128)(2,1)}, u32[]{:S(2)}) copy-start(bf16[3,3,32,32]{3,2,1,0:T(8,128)(2,1)} %param.36) | copy-start | bytes 55300
  71.2 1.8 %copy-start.16 = (bf16[3,3,64,32]{2,3,1,0:T(8,128)(2,1)S(1)}, bf16[3,3,64,32]{2,3,1,0:T(8,128)(2,1)}, u32[]{:S(2)}) copy-start(bf16[3,3,64,32]{2,3,1,0:T(8,128)(2,1)} %param.38) | copy-start | bytes 110596
  71.6 1.7 %copy-start.17 = (bf16[32,64]{1,0:T(8,128)(2,1)S(1)}, bf16[32,64]{1,0:T(8,128)(2,1)}, u32[]{:S(2)}) copy-start(bf16[32,64]{1,0:T(8,128)(2,1)} %param.42) | copy-start | bytes 12292
  71.6 1.8 %copy-start.18 = (bf16[32,32]{1,0:T(8,128)(2,1)S(1)}, bf16[32,32]{1,0:T(8,128)(2,1)}, u32[]{:S(2)}) copy-start(bf16[32,32]{1,0:T(8,128)(2,1)} %param.43) | copy-start | bytes 6148
  71.6 2.0 %copy-start.20 = (bf16[3,3,1,32]{3,1,2,0:T(4,128)(2,1)S(1)}, bf16[3,3,1,32]{3,1,2,0:T(4,128)(2,1)}, u32[]{:S(2)}) copy-start(bf16[3,3,1,32]{3,1,2,0:T(4,128)(2,1)} %param.47) | copy-start | bytes 1732
  71.7 2.1 %copy-start.19 = (bf16[3,3,32,2]{2,3,1,0:T(2,128)(2,1)S(1)}, bf16[3,3,32,2]{2,3,1,0:T(2,128)(2,1)}, u32[]{:S(2)}) copy-start(bf16[3,3,32,2]{2,3,1,0:T(2,128)(2,1)} %param.34) | copy-start | bytes 3460
  71.8 2.2 %copy-start.21 = (f32[32]{0:T(128)S(1)}, f32[32]{0:T(128)}, u32[]{:S(2)}) copy-start(f32[32]{0:T(128)} %param.35) | copy-start | bytes 388
  71.8 2.3 %copy-start.22 = (f32[32]{0:T(128)S(1)}, f32[32]{0:T(128)}, u32[]{:S(2)}) copy-start(f32[32]{0:T(128)} %param.37) | copy-start | bytes 388
  71.8 2.4 %copy-start.23 = (f32[32]{0:T(128)S(1)}, f32[32]{0:T(128)}, u32[]{:S(2)}) copy-start(f32[32]{0:T(128)} %param.44) | copy-start | bytes 388
  71.8 2.4 %copy-start.24 = (f32[32]{0:T(128)S(1)}, f32[32]{0:T(128)}, u32[]{:S(2)}) copy-start(f32[32]{0:T(128)} %param.46) | copy-start | bytes 388
  71.8 2.5 %copy-start.25 = (f32[64]{0:T(128)S(1)}, f32[64]{0:T(128)}, u32[]{:S(2)}) copy-start(f32[64]{0:T(128)} %param.39) | copy-start | bytes 772
  71.8 2.6 %copy-start.26 = (f32[64]{0:T(128)S(1)}, f32[64]{0:T(128)}, u32[]{:S(2)}) copy-start(f32[64]{0:T(128)} %param.41) | copy-start | bytes 772
  71.8 2.7 %copy-start.4 = (f32[128,256]{1,0:T(8,128)S(1)}, f32[128,256]{1,0:T(8,128)}, u32[]{:S(2)}) copy-start(f32[128,256]{1,0:T(8,128)} %sky.3) | copy-start | bytes 393220
  71.8 2.7 %copy-start.6 = (bf16[320,384]{1,0:T(8,128)(2,1)S(1)}, bf16[320,384]{1,0:T(8,128)(2,1)}, u32[]{:S(2)}) copy-start(bf16[320,384]{1,0:T(8,128)(2,1)} %constant.31.clone.into) | copy-start | bytes 737284
  71.9 2.7 %copy-start.7 = (bf16[256,288]{1,0:T(8,128)(2,1)S(1)}, bf16[256,288]{1,0:T(8,128)(2,1)}, u32[]{:S(2)}) copy-start(bf16[256,288]{1,0:T(8,128)(2,1)} %constant.32.clone.back) | copy-start | bytes 442372
  71.9 2.7 %copy-start.9 = (bf16[128,128]{1,0:T(8,128)(2,1)S(1)}, bf16[128,128]{1,0:T(8,128)(2,1)}, u32[]{:S(2)}) copy-start(bf16[128,128]{1,0:T(8,128)(2,1)} %constant.30.clone.eye) | copy-start | bytes 98308

commit v2 on v1

v2 whole, which is shorter than its diff:
```python
import functools
import math

import jax
import jax.numpy as jnp
import numpy as np
from jax import lax
from jax.experimental import pallas as pl
from jax.experimental.pallas import tpu as pltpu
from jax.sharding import PartitionSpec as P

MESH = pl.DeviceIdType.MESH
F32 = jnp.float32
BF16 = jnp.bfloat16

GE, GC, GM, GD, GO = 6, 6, 6, 6, 4
NX, NY = 32, 16
SLABS = 18
STRIPES = 16
PIX = SLABS * STRIPES
PIX2 = PIX // 2
GROUPS = 18


def dot(a, b):
    return jnp.dot(a, b, preferred_element_type=F32)


def dot_nt(a, b):
    return lax.dot_general(a, b, (((1,), (1,)), ((), ())), preferred_element_type=F32)


def complex_block(c, s):
    return np.stack([np.stack([c, -s]), np.stack([s, c])])


def transform_constants():
    turn = 2.0 * math.pi
    y0 = np.arange(128)
    cells = np.arange(256)
    ang = turn * (np.outer(y0, y0) % 128) / 128
    first = complex_block(np.cos(ang), np.sin(ang))
    first = first.reshape(2, 2, 128, 16, 8).transpose(0, 2, 3, 1, 4).reshape(256, 256)
    ang = turn * np.outer(y0, cells % 32) / 4096
    sign = np.where(y0 % 2 == 0, 1.0, -1.0)[:, None]
    twist1 = np.stack([np.cos(ang) * sign, np.sin(ang) * sign])
    short = np.arange(32)
    ang = turn * (np.outer(short, short) % 32) / 32
    c32, s32 = np.cos(ang), np.sin(ang)
    second = complex_block(c32, s32)
    second = np.einsum("abys,rt->yarbts", second, np.eye(8)).reshape(512, 512)
    third = complex_block(c32, s32)
    third = np.einsum("abxi,yz->ayxibz", third, np.eye(8)).reshape(512, 512)
    ang = turn * np.outer(y0, y0) / 4096
    twist2 = np.stack([np.cos(ang) * sign, np.sin(ang) * sign]) / 4096
    ang = turn * (np.outer(short, y0) % 32) / 32
    fourth = np.concatenate([np.cos(ang), -np.sin(ang)], axis=1)
    return (
        jnp.asarray(first, BF16),
        jnp.asarray(twist1, F32),
        jnp.asarray(second, BF16),
        jnp.asarray(third, BF16),
        jnp.asarray(twist2, F32),
        jnp.asarray(fourth, BF16),
        jnp.asarray(np.eye(128), BF16),
    )


def permutations():
    into = np.zeros((20, STRIPES, 384), np.float32)
    back = np.zeros((256, SLABS, STRIPES), np.float32)
    for w in range(-1, SLABS + 1):
        for s in range(STRIPES):
            col = SLABS * s + w - 8
            if 0 <= col < 264:
                into[w + 1, s, col] = 1
            elif -8 <= col < 0:
                into[w + 1, s, 384 + col] = 1
            if 0 <= col < 256 and 0 <= w < SLABS:
                back[col, w, s] = 1
    return jnp.asarray(into.reshape(320, 384), BF16), jnp.asarray(back.reshape(256, PIX), BF16)


def send_all(axis, count, me, source, landing, send_sem, recv_sem):
    def one(step, carry):
        other = lax.rem(me + step, count)
        pltpu.make_async_remote_copy(
            src_ref=source.at[other],
            dst_ref=landing.at[me],
            send_sem=send_sem,
            recv_sem=recv_sem,
            device_id={axis: other},
            device_id_type=MESH,
        ).start()
        return carry

    lax.fori_loop(1, count, one, 0)
    landing[me] = source[me]


def wait_bytes(ref, sem):
    pltpu.make_async_copy(ref, ref, sem).wait()


def grid_tiles(vis, counts, owner, kernels):
    wide = vis[...].astype(F32)
    parts = [jnp.concatenate([wide[:, k, :]] * 2, axis=1) for k in range(2)]
    slot = lax.broadcasted_iota(jnp.int32, (64, 128), 0)
    half = lax.broadcasted_iota(jnp.int32, (64, 128), 1) // 64
    contrib = None
    for piece in range(8):
        blocks = []
        for q in range(4 * piece, 4 * piece + 4):
            hit = slot == 2 * q + half
            block = [jnp.where(hit, part, 0.0).astype(BF16) for part in parts]
            blocks.append(jnp.concatenate(block, axis=0))
        term = dot(jnp.concatenate(blocks, axis=1), kernels[512 * piece : 512 * piece + 512, :])
        contrib = term if contrib is None else contrib + term
    live = jnp.sum(counts[...], axis=1, keepdims=True)
    both = jnp.concatenate([owner[...]] * 2, axis=1)
    lane = lax.broadcasted_iota(jnp.int32, (1, 128), 1) % 64
    both = jnp.where(lane < live, both, -1)
    chosen = jnp.where(lax.broadcasted_iota(jnp.int32, (128, 128), 0) == both, 1.0, 0.0)
    chosen = chosen.astype(BF16)
    sums = []
    for k in range(2):
        own = contrib[64 * k : 64 * k + 64]
        high = own.astype(BF16)
        low = (own - high.astype(F32)).astype(BF16)
        total = dot(chosen, jnp.concatenate([high, low], axis=0))
        sums.append(total.reshape(16, 8, 256))
    return jnp.concatenate(sums, axis=1).astype(BF16)


def column_transform(held, first, twist1, second):
    turned = dot(first[...], held)
    real, imag = turned[:128], turned[128:]
    c, s = twist1[0], twist1[1]
    both = jnp.concatenate([real * c - imag * s, real * s + imag * c], axis=1).astype(BF16)
    return dot_nt(second[...], both)


def columns_up(held, eye):
    wide = held.astype(F32).reshape(16, 4, 8, 128)
    halves = []
    for y1 in range(2):
        parts = []
        for part in range(2):
            piece = wide[:, 2 * y1 + part].reshape(128, 128).astype(BF16)
            parts.append(dot_nt(eye, piece).reshape(16, 8, 128))
        halves.append(jnp.concatenate(parts, axis=1))
    return jnp.concatenate(halves, axis=0).astype(BF16)


def row_transform(held, third, twist2, fourth, store):
    turned = dot(third[...], held)
    for y in range(8):
        real = turned[32 * y : 32 * y + 32]
        imag = turned[256 + 32 * y : 256 + 32 * y + 32]
        real = jnp.concatenate([real] * 4, axis=0)
        imag = jnp.concatenate([imag] * 4, axis=0)
        c, s = twist2[0], twist2[1]
        both = jnp.concatenate([real * c - imag * s, real * s + imag * c], axis=1).astype(BF16)
        store(y, dot_nt(fourth[...], both))


def repeat_matrix(rows):
    row = lax.broadcasted_iota(jnp.int32, (rows, 256), 0)
    lane = lax.broadcasted_iota(jnp.int32, (rows, 256), 1)
    return jnp.where(lane % rows == row, 1.0, 0.0).astype(BF16)


def dot_tn(a, b):
    return lax.dot_general(a, b, (((0,), (0,)), ((), ())), preferred_element_type=F32)


def band(dst, tile, high, rows, start, lane_id, count):
    for dc in range(3):
        taps = [tile(p, dc) for p in range(3)]
        for row in range(rows):
            block = None
            for p in range(3):
                out_row = row - start - p
                if 0 <= out_row < count:
                    term = jnp.where(lane_id == out_row, taps[p], 0.0)
                    block = term if block is None else block + term
            if block is None:
                block = jnp.zeros(lane_id.shape, F32)
            at = (dc * rows + row) * high
            dst[at : at + high, :] = block.astype(BF16)


def exchange_kernel(*refs):
    (
        first_h,
        twist1_h,
        second_h,
        third_h,
        twist2_h,
        fourth_h,
        eye_h,
        kernels_h,
        vis_h,
        counts_h,
        owner_h,
        sky_h,
    ) = refs[:12]
    weights_h = refs[12:26]
    dirty_out, rows_out, cols_out = refs[26:29]
    bands_out = refs[29:38]
    (
        first,
        twist1,
        second,
        third,
        twist2,
        fourth,
        eye,
        kernels,
        vis,
        counts,
        owner,
        sky,
    ) = refs[38:50]
    weights = refs[50:64]
    built = refs[64:73]
    w_enter, w_encode, w_coarse, w_deeper, w_decode, w_output, w_upward, w_skip, biases = built
    (
        tiles,
        landed1,
        bands,
        landed2,
        ups,
        landed3,
        image,
        downs,
        landed4,
        sides,
        sky_rows,
        sky_sides,
        sky_cols,
        sky_own,
        send_sem,
        recv_sem,
        load_sem,
        save_sem,
    ) = refs[73:]
    saves = [
        pltpu.make_async_copy(source, target, save_sem.at[k])
        for k, (source, target) in enumerate(zip(built, bands_out))
    ]
    save_rows = pltpu.make_async_copy(sky_rows, rows_out, save_sem.at[9])
    save_cols = pltpu.make_async_copy(sky_sides, cols_out, save_sem.at[10])
    save_main = pltpu.make_async_copy(landed4, dirty_out.at[pl.ds(0, 32)], save_sem.at[11])
    save_sides = pltpu.make_async_copy(sides, dirty_out.at[pl.ds(32, 2)], save_sem.at[12])
    gx, gy = lax.axis_index("gx"), lax.axis_index("gy")
    down_x, up_x = lax.rem(gx + 1, NX), lax.rem(gx + NX - 1, NX)
    right_y, left_y = lax.rem(gy + 1, NY), lax.rem(gy + NY - 1, NY)
    barrier = pltpu.get_barrier_semaphore()

    def greet(axis, count, me):
        def one(step, carry):
            pl.semaphore_signal(
                barrier, inc=1, device_id={axis: lax.rem(me + step, count)}, device_id_type=MESH
            )
            return carry

        lax.fori_loop(1, count, one, 0)

    greet("gy", NY, gy)
    greet("gx", NX, gx)
    for x, y in ((NX - 1, left_y), (0, right_y)):
        pl.semaphore_signal(barrier, inc=1, device_id={"gx": x, "gy": y}, device_id_type=MESH)

    sources = (kernels_h, vis_h, counts_h, owner_h, sky_h, first_h, twist1_h, second_h)
    sources += weights_h + (third_h, twist2_h, fourth_h, eye_h)
    targets = (kernels, vis, counts, owner, sky, first, twist1, second)
    targets += weights + (third, twist2, fourth, eye)
    loads = [
        pltpu.make_async_copy(source, target, load_sem.at[k])
        for k, (source, target) in enumerate(zip(sources, targets))
    ]
    for load in loads:
        load.start()

    for load in loads[:5]:
        load.wait()
    sky_own[...] = sky[...].astype(BF16)
    tiles[...] = grid_tiles(vis, counts, owner, kernels)
    edge = jnp.where((gx == 0) | (gx == NX - 1), NX, 0)
    pl.semaphore_wait(barrier, NX + NY - 2 + edge)

    send_all("gy", NY, gy, tiles, landed1, send_sem.at[0], recv_sem.at[0])

    def to_side(source, target, slot, axis, other):
        return pltpu.make_async_remote_copy(
            src_ref=source,
            dst_ref=target,
            send_sem=send_sem.at[slot],
            recv_sem=recv_sem.at[slot],
            device_id={axis: other},
            device_id_type=MESH,
        )

    row_copies = [
        to_side(sky_own.at[pl.ds(112, 16)], sky_rows.at[0], 4, "gx", down_x),
        to_side(sky_own.at[pl.ds(0, 16)], sky_rows.at[1], 5, "gx", up_x),
    ]
    for copy in row_copies:
        copy.start()

    for load in loads[5:]:
        load.wait()
    enter_w, encode_w, coarse_w, deeper_w, decode_w, output_w, upward_w, skip_w = weights[:8]
    rep32, rep64 = repeat_matrix(32), repeat_matrix(64)
    lane32 = lax.broadcasted_iota(jnp.int32, (32, 256), 1)
    lane64 = lax.broadcasted_iota(jnp.int32, (64, 256), 1)
    band(w_encode, lambda p, dc: dot_tn(encode_w[p, dc], rep32), 32, 16, 3, lane32 // 32, 8)
    saves[1].start()
    band(w_decode, lambda p, dc: dot_tn(decode_w[p, dc], rep32), 32, 16, 3, lane32 // 32, 8)
    saves[4].start()

    wait_bytes(landed1.at[pl.ds(0, 15)], recv_sem.at[0])
    turned = column_transform(landed1[...].reshape(256, 256), first, twist1, second)
    bands[...] = turned.astype(BF16).reshape(16, 32, 128)
    send_all("gy", NY, gy, bands, landed2, send_sem.at[1], recv_sem.at[1])

    for copy in row_copies:
        copy.wait()
    for half in range(2):
        lanes = slice(128 * half, 128 * half + 128)
        sky_cols[half, 0:16] = sky_rows[0, :, lanes]
        sky_cols[half, 16:144] = sky_own[:, lanes]
        sky_cols[half, 144:160] = sky_rows[1, :, lanes]
    col_copies = [
        to_side(sky_cols.at[1], sky_sides.at[0], 6, "gy", right_y),
        to_side(sky_cols.at[0], sky_sides.at[1], 7, "gy", left_y),
    ]
    for copy in col_copies:
        copy.start()

    band(w_coarse, lambda p, dc: dot(coarse_w[p, dc], rep64), 32, 12, 3, lane32 // 64, 4)
    saves[2].start()
    band(w_deeper, lambda p, dc: dot_tn(deeper_w[p, dc], rep64), 64, 8, 1, lane64 // 64, 4)
    saves[3].start()
    lane_out = lax.broadcasted_iota(jnp.int32, (32, 128), 1)
    tap_row = lax.broadcasted_iota(jnp.int32, (3, 128), 0)

    def output_tile(p, dc):
        return dot_tn(output_w[p], jnp.where(tap_row == dc, 1.0, 0.0).astype(BF16))

    band(w_output, output_tile, 32, 16, 3, lane_out % 8, 8)
    saves[5].start()

    wait_bytes(landed2.at[pl.ds(0, 15)], recv_sem.at[1])
    ups[...] = columns_up(landed2[...], eye[...])
    send_all("gx", NX, gx, ups, landed3, send_sem.at[2], recv_sem.at[2])

    lifted = dot_tn(upward_w[...], rep32)
    for row in range(4):
        block = jnp.where(lane64 // 64 == row, lifted, 0.0)
        w_upward[64 * row : 64 * row + 64, :] = block.astype(BF16)
    skipped = dot_tn(skip_w[...], rep32)
    for row in range(8):
        block = jnp.where(lane32 // 32 == row, skipped, 0.0)
        w_skip[32 * row : 32 * row + 32, :] = block.astype(BF16)
    row_id = lax.broadcasted_iota(jnp.int32, (64, 256), 0)
    for dc in range(3):
        taps = [dot(enter_w[p, dc], rep32) for p in range(3)]
        for variant in range(4):
            for channel in range(2):
                block = jnp.zeros((64, 256), F32)
                for p in range(3):
                    hit = row_id - 15 - 8 * variant - p == lane64 // 32
                    block = block + jnp.where(hit, taps[p][channel : channel + 1, :], 0.0)
                at = dc * 128 + channel * 64
                w_enter[variant, at : at + 64, :] = block.astype(BF16)
    for row, ref in enumerate(weights[8:]):
        biases[row : row + 1, :] = jnp.concatenate([ref[...]] * (256 // ref.shape[1]), axis=1)
    biases[6:8, :] = jnp.zeros((2, 256), F32)
    for k in (0, 6, 7, 8):
        saves[k].start()

    def store(y, value):
        image[pl.ds(8 + y, 32, stride=8), :] = value

    image[0:8] = jnp.zeros((8, 128), F32)
    image[264:272] = jnp.zeros((8, 128), F32)

    wait_bytes(landed3.at[pl.ds(0, 31)], recv_sem.at[2])
    row_transform(landed3[...].reshape(512, 128), third, twist2, fourth, store)
    whole = image[...].reshape(34, 8, 128)
    lane = lax.broadcasted_iota(jnp.int32, (32, 8, 128), 2)
    outer = jnp.where(lane < 64, whole[2:34], whole[0:32])
    downs[...] = jnp.concatenate([whole[1:33], outer], axis=1).astype(BF16)
    send_all("gx", NX, gx, downs, landed4, send_sem.at[3], recv_sem.at[3])

    def beside(other_y, slot):
        def one(x, carry):
            pltpu.make_async_remote_copy(
                src_ref=downs.at[x],
                dst_ref=sides.at[slot],
                send_sem=send_sem.at[8 + slot],
                recv_sem=recv_sem.at[8 + slot],
                device_id={"gx": x, "gy": other_y},
                device_id_type=MESH,
            ).start()
            return carry

        lax.fori_loop(0, NX, one, 0)

    @pl.when(gx == NX - 1)
    def _():
        beside(right_y, 0)

    @pl.when(gx == 0)
    def _():
        beside(left_y, 1)

    for copy in col_copies:
        copy.wait()
    save_rows.start()
    save_cols.start()

    wait_bytes(landed4.at[pl.ds(0, 31)], recv_sem.at[3])
    save_main.start()
    wait_bytes(sides.at[0], recv_sem.at[8])
    wait_bytes(sides.at[1], recv_sem.at[9])
    save_sides.start()
    for save in saves + [save_rows, save_cols]:
        save.wait()
    save_main.wait()
    save_sides.wait()
    wait_bytes(tiles.at[pl.ds(0, 15)], send_sem.at[0])
    wait_bytes(bands.at[pl.ds(0, 15)], send_sem.at[1])
    wait_bytes(ups.at[pl.ds(0, 31)], send_sem.at[2])
    wait_bytes(downs.at[pl.ds(0, 31)], send_sem.at[3])

    @pl.when(gx == NX - 1)
    def _():
        wait_bytes(downs, send_sem.at[8])

    @pl.when(gx == 0)
    def _():
        wait_bytes(downs, send_sem.at[9])


def exchange(vis, counts, owner, kernels, sky, weights):
    hbm = pl.BlockSpec(memory_space=pltpu.HBM)
    operands = transform_constants() + (kernels, vis, counts, owner, sky) + weights
    shapes = [
        (34, 16, 128),
        (2, 16, 256),
        (2, 160, 128),
        (4, 384, 256),
        (1536, 256),
        (1152, 256),
        (1536, 256),
        (1536, 256),
        (1536, 128),
        (256, 256),
        (256, 256),
    ]
    outs = [jax.ShapeDtypeStruct(shape, BF16) for shape in shapes]
    outs.append(jax.ShapeDtypeStruct((8, 256), F32))
    return pl.pallas_call(
        exchange_kernel,
        out_shape=tuple(outs),
        in_specs=[hbm] * len(operands),
        out_specs=(hbm,) * len(outs),
        scratch_shapes=[pltpu.VMEM(x.shape, x.dtype) for x in list(operands) + outs[3:]]
        + [
            pltpu.VMEM((16, 16, 256), BF16),
            pltpu.VMEM((16, 16, 256), BF16),
            pltpu.VMEM((16, 32, 128), BF16),
            pltpu.VMEM((16, 32, 128), BF16),
            pltpu.VMEM((32, 16, 128), BF16),
            pltpu.VMEM((32, 16, 128), BF16),
            pltpu.VMEM((272, 128), F32),
            pltpu.VMEM((32, 16, 128), BF16),
            pltpu.VMEM((32, 16, 128), BF16),
            pltpu.VMEM((2, 16, 128), BF16),
            pltpu.VMEM((2, 16, 256), BF16),
            pltpu.VMEM((2, 160, 128), BF16),
            pltpu.VMEM((2, 160, 128), BF16),
            pltpu.VMEM((128, 256), BF16),
            pltpu.SemaphoreType.DMA((10,)),
            pltpu.SemaphoreType.DMA((10,)),
            pltpu.SemaphoreType.DMA((len(operands),)),
            pltpu.SemaphoreType.DMA((13,)),
        ],
        compiler_params=pltpu.CompilerParams(
            collective_id=0, has_side_effects=True, vmem_limit_bytes=64 << 20
        ),
        name="exchange",
    )(*operands)


def network_kernel(*refs):
    sources, (dirty_out, estimate_out), targets = refs[:16], refs[16:18], refs[18:34]
    window, entry, fine_a, fine_b, fine_c, pooled, coarse, mask, w_pool, drawn, load_sem = refs[34:]
    loads = [
        pltpu.make_async_copy(source, target, load_sem.at[k])
        for k, (source, target) in enumerate(zip(sources, targets))
    ]
    for load in loads:
        load.start()
    sky, dirty_in, rows_in, cols_in, eye, into, w_enter, biases = targets[:8]
    w_encode, w_coarse, w_deeper, w_upward, w_skip, w_decode, w_output, back = targets[8:]

    def arrived(first, last):
        for load in loads[first:last]:
            load.wait()

    gx, gy = lax.axis_index("gx"), lax.axis_index("gy")
    last_x, last_y = lax.axis_size("gx") - 1, lax.axis_size("gy") - 1
    keep_top = jnp.where(gx == 0, 0.0, 1.0).astype(F32)
    keep_bottom = jnp.where(gx == last_x, 0.0, 1.0).astype(F32)

    rows512 = lax.broadcasted_iota(jnp.int32, (512, 128), 0)
    lanes512 = lax.broadcasted_iota(jnp.int32, (512, 128), 1)
    pairs = ((rows512 % 256) // 64 == lanes512 // 32) & (rows512 % 32 == lanes512 % 32)
    w_pool[...] = jnp.where(pairs, 0.25, 0.0).astype(BF16)
    slab = lax.broadcasted_iota(jnp.int32, (20, 16, 128), 0)
    stripe = lax.broadcasted_iota(jnp.int32, (20, 16, 128), 1)
    col = SLABS * stripe + slab - 9 + 256 * gy
    mask[...] = jnp.where((col >= 0) & (col < 256 * (last_y + 1)), 1.0, 0.0).astype(F32)

    arrived(0, 6)
    lane = lax.broadcasted_iota(jnp.int32, (160, 128), 1)
    beside = jnp.where(lane < 64, cols_in[1].astype(F32), cols_in[0].astype(F32))
    above = rows_in[0].astype(F32)[8:16] * keep_top
    below = rows_in[1].astype(F32)[0:8] * keep_bottom
    zeros = jnp.zeros((32, 256), F32)
    window[0, :, 0:256] = jnp.concatenate(
        [zeros[:16], above, sky[...], below, zeros], axis=0
    ).astype(BF16)
    beside = jnp.concatenate(
        [
            zeros[:16, :128],
            beside[8:16] * keep_top,
            beside[16:144],
            beside[144:152] * keep_bottom,
            zeros[:, :128],
        ],
        axis=0,
    )
    window[0, :, 256:384] = beside.astype(BF16)
    wide = dirty_in[...].astype(F32)
    gap = jnp.zeros((112, 128), F32)
    parts = []
    for half in range(2):
        rows8 = slice(8 * half, 8 * half + 8)
        stacked = jnp.concatenate(
            [wide[0:32, rows8].reshape(256, 128), wide[33, rows8], gap, wide[32, rows8]], axis=0
        )
        parts.append(dot_nt(eye[...], stacked.astype(BF16)))
    dirty_out[...] = parts[0][:, 0:256]
    zeros = jnp.zeros((32, 384), F32)
    window[1] = jnp.concatenate(
        [zeros[:16], parts[1][120:128] * keep_top, parts[0], parts[1][0:8] * keep_bottom, zeros],
        axis=0,
    ).astype(BF16)
    for q in range(5):
        rows64 = slice(32 * q, 32 * q + 64)
        both = jnp.concatenate([window[0, rows64], window[1, rows64]], axis=0)
        placed = dot_nt(into[...], both).reshape(20, 16, 128) * mask[...]
        entry[q] = placed.astype(BF16)

    blank = jnp.zeros((20, 16, 128), BF16)
    for ref, top in ((fine_a, 37), (fine_b, 37), (fine_c, 37), (pooled, 19), (coarse, 37)):
        ref[0] = blank[: ref.shape[1]]
        ref[top] = blank[: ref.shape[1]]

    def row_keep(group):
        top = jnp.where(group == 0, keep_top, 1.0)
        bottom = jnp.where(group == GROUPS - 1, keep_bottom, 1.0)
        return top * bottom

    def put(ref, at, value, slabs):
        ref[at, 1 : slabs + 1] = value.astype(BF16)
        ref[at, 0] = pltpu.roll(value[slabs - 1], 1, 0).astype(BF16)
        ref[at, slabs + 1] = pltpu.roll(value[0], STRIPES - 1, 0).astype(BF16)

    def finish(total, bias_row, keep):
        value = jnp.maximum(total + biases[bias_row : bias_row + 1, :], 0.0)
        scaled = mask[1:19] * keep
        return [
            value[:, 128 * h : 128 * h + 128].reshape(SLABS, 16, 128) * scaled for h in range(2)
        ]

    def gathered(ref, at, high, slabs, stride, count):
        pieces = []
        for dc in range(3):
            for h in range(high):
                rows = [
                    ref[at + stride * g + h, dc : dc + slabs].reshape(slabs * 16, 128)
                    for g in range(count)
                ]
                pieces.append(jnp.concatenate(rows, axis=0))
        return jnp.concatenate(pieces, axis=1)

    arrived(6, 8)
    for variant in range(4):
        members = list(range(variant, GROUPS, 4))
        pieces = []
        for dc in range(3):
            rows = [entry[group // 4, dc : dc + SLABS].reshape(PIX, 128) for group in members]
            pieces.append(jnp.concatenate(rows, axis=0))
        total = dot(jnp.concatenate(pieces, axis=1), w_enter[variant])
        for g, group in enumerate(members):
            for h, value in enumerate(finish(total[PIX * g : PIX * g + PIX], 0, row_keep(group))):
                put(fine_a, 2 * group + 1 + h, value, SLABS)

    def encode_step(step, carry):
        total = dot(gathered(fine_a, 2 * GE * step, 4, SLABS, 2, GE), w_encode[...])
        columns = [[], [], [], []]
        for g in range(GE):
            group = GE * step + g
            for h, value in enumerate(finish(total[PIX * g : PIX * g + PIX], 1, row_keep(group))):
                put(fine_b, 2 * group + 1 + h, value, SLABS)
                split = value.reshape(SLABS // 2, 2, 16, 128)
                columns[h].append(split[:, 0].reshape(PIX2, 128).astype(BF16))
                columns[2 + h].append(split[:, 1].reshape(PIX2, 128).astype(BF16))
        both = jnp.concatenate([jnp.concatenate(c, axis=0) for c in columns], axis=1)
        small = dot(both, w_pool[...])
        for g in range(GE):
            value = small[PIX2 * g : PIX2 * g + PIX2].reshape(SLABS // 2, 16, 128)
            put(pooled, GE * step + g + 1, value, SLABS // 2)
        return carry

    arrived(8, 9)
    lax.fori_loop(0, GROUPS // GE, encode_step, 0)

    even_mask = mask[1:19].reshape(SLABS // 2, 2, 16, 128)[:, 0]

    def coarse_step(step, carry):
        total = dot(gathered(pooled, GC * step, 3, SLABS // 2, 1, GC), w_coarse[...])
        for g in range(GC):
            group = GC * step + g
            value = jnp.maximum(total[PIX2 * g : PIX2 * g + PIX2] + biases[2:3, :], 0.0)
            scaled = even_mask * row_keep(group)
            for h in range(2):
                half = value[:, 128 * h : 128 * h + 128].reshape(SLABS // 2, 16, 128) * scaled
                put(coarse, 2 * group + 1 + h, half, SLABS // 2)
        return carry

    arrived(9, 10)
    lax.fori_loop(0, GROUPS // GC, coarse_step, 0)

    def merge_step(step, carry):
        total = dot(gathered(coarse, 2 * GM * step, 4, SLABS // 2, 2, GM), w_deeper[...])
        value = jnp.maximum(total + biases[3:4, :], 0.0).astype(BF16)
        lifted = dot(value, w_upward[...]).reshape(GM, SLABS // 2, 1, 16, 256)
        halves = []
        for h in range(2):
            rows = [
                fine_b[2 * (GM * step + g) + 1 + h, 1:19].reshape(PIX, 128) for g in range(GM)
            ]
            halves.append(jnp.concatenate(rows, axis=0))
        skipped = dot(jnp.concatenate(halves, axis=1), w_skip[...])
        total = skipped.reshape(GM, SLABS // 2, 2, 16, 256) + lifted
        total = total.reshape(GM * PIX, 256)
        for g in range(GM):
            group = GM * step + g
            for h, half in enumerate(finish(total[PIX * g : PIX * g + PIX], 4, row_keep(group))):
                put(fine_a, 2 * group + 1 + h, half, SLABS)
        return carry

    arrived(10, 13)
    lax.fori_loop(0, GROUPS // GM, merge_step, 0)

    def decode_step(step, carry):
        total = dot(gathered(fine_a, 2 * GD * step, 4, SLABS, 2, GD), w_decode[...])
        for g in range(GD):
            group = GD * step + g
            for h, half in enumerate(finish(total[PIX * g : PIX * g + PIX], 5, row_keep(group))):
                put(fine_c, 2 * group + 1 + h, half, SLABS)
        return carry

    arrived(13, 14)
    lax.fori_loop(0, GROUPS // GD, decode_step, 0)

    lane_row = lax.broadcasted_iota(jnp.int32, (PIX, 128), 1) // 8

    def output_step(step, carry):
        total = dot(gathered(fine_c, 2 + 2 * GO * step, 4, SLABS, 2, GO), w_output[...])
        kept = drawn[...]
        for g in range(GO):
            kept = jnp.where(lane_row == GO * step + g, total[PIX * g : PIX * g + PIX], kept)
        drawn[...] = kept
        return carry

    drawn[...] = jnp.zeros((PIX, 128), F32)
    arrived(14, 16)
    lax.fori_loop(0, 16 // GO, output_step, 0)

    update = drawn[...]
    high = update.astype(BF16)
    low = (update - high.astype(F32)).astype(BF16)
    ordered = dot(back[...], high) + dot(back[...], low)
    estimate_out[...] = sky[...] + ordered.T


def network(sky, dirty_in, rows_in, cols_in, bands):
    vmem, hbm = pl.BlockSpec(memory_space=pltpu.VMEM), pl.BlockSpec(memory_space=pltpu.HBM)
    into, back = permutations()
    eye = jnp.asarray(np.eye(128), BF16)
    enter, encode, coarse, deeper, decode, output, upward, skip, biases = bands
    operands = (sky, dirty_in, rows_in, cols_in, eye, into, enter, biases)
    operands += (encode, coarse, deeper, upward, skip, decode, output, back)
    return pl.pallas_call(
        network_kernel,
        out_shape=(
            jax.ShapeDtypeStruct((128, 256), F32),
            jax.ShapeDtypeStruct((128, 256), F32),
        ),
        in_specs=[hbm] * len(operands),
        out_specs=(vmem, vmem),
        scratch_shapes=[pltpu.VMEM(x.shape, x.dtype) for x in operands]
        + [
            pltpu.VMEM((2, 192, 384), BF16),
            pltpu.VMEM((5, 20, 16, 128), BF16),
            pltpu.VMEM((38, 20, 16, 128), BF16),
            pltpu.VMEM((38, 20, 16, 128), BF16),
            pltpu.VMEM((38, 20, 16, 128), BF16),
            pltpu.VMEM((20, 11, 16, 128), BF16),
            pltpu.VMEM((38, 11, 16, 128), BF16),
            pltpu.VMEM((20, 16, 128), F32),
            pltpu.VMEM((512, 128), BF16),
            pltpu.VMEM((PIX, 128), F32),
            pltpu.SemaphoreType.DMA((len(operands),)),
        ],
        compiler_params=pltpu.CompilerParams(vmem_limit_bytes=64 << 20),
        name="network",
    )(*operands)


def raw_weights(ew, eb, nw, nb, cw, cb, dw, db, uw, sw, mb, ow, ob, fw):
    biases = tuple(b.reshape(1, -1) for b in (eb, nb, cb, db, mb, ob))
    return (
        jnp.swapaxes(ew, 2, 3),
        nw,
        jnp.swapaxes(cw, 2, 3),
        dw,
        ow,
        fw[:, :, 0, :],
        uw,
        sw,
    ) + biases


def shards(
    sky_image,
    visibilities,
    grid_kernels,
    tile_counts,
    block_tiles,
    *parameters,
):
    slots = block_tiles.shape[2]
    dirty, rows, cols, *bands = exchange(
        visibilities[0, 0],
        tile_counts.reshape(1, -1),
        block_tiles.reshape(1, -1),
        grid_kernels.reshape(slots * 64, 256),
        sky_image,
        raw_weights(*parameters),
    )
    return network(sky_image, dirty, rows, cols, tuple(bands))


def solution(mesh):
    block = P("gx", "gy")
    return jax.shard_map(
        shards,
        mesh=mesh,
        in_specs=(
            block,
            P("gx", "gy", None, None, None),
            P("gx", "gy", None, None, None),
            P("gx", "gy", None),
            P("gx", "gy", None),
        )
        + (P(),) * 14,
        out_specs=(block, block),
        check_vma=False,
    )
```

time: 121 us -> 85.3 us (0.70)
  Pallas kernels: 104 us -> 84.6 us
  local copies, waits for them, and re-layouts: 13.2 us -> 0 us
  other arithmetic: 2.63 us -> 0 us
    pallas_call x1, Pallas kernels: 46.2 us -> 27.5 us  [network(): pl.pallas_call(network_kernel, out_shape=(jax.ShapeDtypeStruct((128, 256)...]
    unnamed x54 -> x0, local copies, waits for them, and re-layouts: 8.91 us -> none
    another operation x32 -> x0, local copies, waits for them, and re-layouts: 2.89 us -> none  [the longest x10 1.92 us: tap_tiles(): turned = jnp.tile(turned, (1, 1, 1, copies))]
    reduce_sum x1 -> x0, other arithmetic: 1.33 us -> none  [shards(): live = jnp.arange(slots, dtype=jnp.int32) < jnp.sum(tile_counts[0, 0])]
    select_n x1 -> x0, other arithmetic: 1.3 us -> none  [shards(): jnp.where(live, block_tiles[0, 0], -1)]
    transpose x5 -> x0, local copies, waits for them, and re-layouts: 1.22 us -> none  [the longest x1 0.77 us: shards(): vis = jnp.swapaxes(visibilities[0, 0], 0, 1).reshape(2, slots * 64)]
where the time goes in v2:
time: 85.3 us; the launch traced here: 85.2 us
  Pallas kernels  84.6 us (99%)
    pallas_call x1, Pallas kernels, exchange(): pl.pallas_call(exchange_kernel, out_shape=tuple(outs), in_specs=[hbm] * l...  57 us
    pallas_call x1, Pallas kernels, network(): pl.pallas_call(network_kernel, out_shape=(jax.ShapeDtypeStruct((128, 256)...  27.5 us

profile of v2, /device:TPU:1, one launch (start us, length us, event | category | flops | bytes accessed | tf_op | source)
XLA Modules:
  0.0 85.2 jit_solution(11454031197227205397)
XLA Ops:
  0.6 57.0 %exchange.1 = (bf16[34,16,128]{2,1,0:T(8,128)(2,1)}, bf16[2,16,256]{2,1,0:T(8,128)(2,1)}, bf16[2,160,128]{2,1,0:T(8,128)(2,1)}, bf16[4,384,256]{2,1,0:T(8,128)(2...) custom-call(bf16[256,256]{1,0:T(8,128)(2,1)} %constant.18.clone.refs, ...), custom_call_target="tpu_custom_call" | custom-call | tf_op jit(solution)/shard_map/exchange/pallas_call | solution.py:466
  57.7 27.5 %network.1 = (f32[128,256]{1,0:T(8,128)}, f32[128,256]{1,0:T(8,128)}) custom-call(f32[128,256]{1,0:T(8,128)} %refs_0_.2, bf16[34,16,128]{2,1,0:T(8,128)(2,1)} %get-tuple-element.14.refs_1_, bf16[2,16,256]{2,1,0:T(8,128)(2,1)} %get-tuple-element.15.refs_2_, bf16[2,160,128]{2,1,0:T(8,128)(2,1)} %get-tuple-element.16.refs_3_, ...), custom_call_target="tpu_custom_call" | custom-call | tf_op jit(solution)/shard_map/network/pallas_call | solution.py:712

commit v3 on v2

--- a/solution.py
+++ b/solution.py
@@ -13,7 +13,7 @@
 F32 = jnp.float32
 BF16 = jnp.bfloat16
 
-GE, GC, GM, GD, GO = 6, 6, 6, 6, 4
+GE, GC, GM, GD = 9, 9, 9, 9
 NX, NY = 32, 16
 SLABS = 18
 STRIPES = 16
@@ -83,7 +83,9 @@
 
 def send_all(axis, count, me, source, landing, send_sem, recv_sem):
     def one(step, carry):
-        other = lax.rem(me + step, count)
+        away = (step + 1) // 2
+        shift = count // 2 + jnp.where(step % 2 == 1, away, -away)
+        other = lax.rem(me + shift, count)
         pltpu.make_async_remote_copy(
             src_ref=source.at[other],
             dst_ref=landing.at[me],
@@ -94,7 +96,7 @@
         ).start()
         return carry
 
-    lax.fori_loop(1, count, one, 0)
+    lax.fori_loop(0, count - 1, one, 0)
     landing[me] = source[me]
 
 
@@ -174,20 +176,40 @@
     return lax.dot_general(a, b, (((0,), (0,)), ((), ())), preferred_element_type=F32)
 
 
-def band(dst, tile, high, rows, start, lane_id, count):
+def band(dst, tile, high, rows, out_row, place, lane_id, count):
     for dc in range(3):
         taps = [tile(p, dc) for p in range(3)]
-        for row in range(rows):
-            block = None
+        for row in rows:
+            block = jnp.zeros(lane_id.shape, F32)
             for p in range(3):
-                out_row = row - start - p
-                if 0 <= out_row < count:
-                    term = jnp.where(lane_id == out_row, taps[p], 0.0)
-                    block = term if block is None else block + term
-            if block is None:
-                block = jnp.zeros(lane_id.shape, F32)
-            at = (dc * rows + row) * high
+                if 0 <= out_row(row, p) < count:
+                    block = block + jnp.where(lane_id == out_row(row, p), taps[p], 0.0)
+            at = place(dc, row)
             dst[at : at + high, :] = block.astype(BF16)
+
+
+def place_fine(dc, row):
+    if row == 3:
+        return (800, 864, 992)[dc]
+    if row == 12:
+        return (832, 768, 896)[dc]
+    return 256 * dc + 32 * (row - 4)
+
+
+def place_coarse(dc, row):
+    if row < 4:
+        return 768 + 128 * dc + 64 + 32 * (row - 2)
+    if row > 11:
+        return 768 + 128 * dc + 32 * (row - 12)
+    return 256 * dc + 32 * (row - 4)
+
+
+def place_deeper(dc, row):
+    if row == 1:
+        return 768 + 128 * dc + 64
+    if row == 6:
+        return 768 + 128 * dc
+    return 256 * dc + 64 * (row - 2)
 
 
 def exchange_kernel(*refs):
@@ -315,10 +337,19 @@
     rep32, rep64 = repeat_matrix(32), repeat_matrix(64)
     lane32 = lax.broadcasted_iota(jnp.int32, (32, 256), 1)
     lane64 = lax.broadcasted_iota(jnp.int32, (64, 256), 1)
-    band(w_encode, lambda p, dc: dot_tn(encode_w[p, dc], rep32), 32, 16, 3, lane32 // 32, 8)
-    saves[1].start()
-    band(w_decode, lambda p, dc: dot_tn(decode_w[p, dc], rep32), 32, 16, 3, lane32 // 32, 8)
-    saves[4].start()
+    rows = range(3, 13)
+
+    def fine_row(row, p):
+        return row - 3 - p
+
+    for dst, raw, save in ((w_encode, encode_w, saves[1]), (w_decode, decode_w, saves[4])):
+        dst[928:992, :] = jnp.zeros((64, 256), BF16)
+
+        def tile(p, dc, raw=raw):
+            return dot_tn(raw[p, dc], rep32)
+
+        band(dst, tile, 32, rows, fine_row, place_fine, lane32 // 32, 8)
+        save.start()
 
     wait_bytes(landed1.at[pl.ds(0, 15)], recv_sem.at[0])
     turned = column_transform(landed1[...].reshape(256, 256), first, twist1, second)
@@ -339,17 +370,33 @@
     for copy in col_copies:
         copy.start()
 
-    band(w_coarse, lambda p, dc: dot(coarse_w[p, dc], rep64), 32, 12, 3, lane32 // 64, 4)
+    def coarse_tile(p, dc):
+        return dot(coarse_w[p, dc], rep64)
+
+    def coarse_row(row, p):
+        return row // 2 - 1 - p
+
+    band(w_coarse, coarse_tile, 32, range(2, 14), coarse_row, place_coarse, lane32 // 64, 4)
     saves[2].start()
-    band(w_deeper, lambda p, dc: dot_tn(deeper_w[p, dc], rep64), 64, 8, 1, lane64 // 64, 4)
+
+    def deeper_tile(p, dc):
+        return dot_tn(deeper_w[p, dc], rep64)
+
+    def deeper_row(row, p):
+        return row - 1 - p
+
+    band(w_deeper, deeper_tile, 64, range(1, 7), deeper_row, place_deeper, lane64 // 64, 4)
     saves[3].start()
-    lane_out = lax.broadcasted_iota(jnp.int32, (32, 128), 1)
-    tap_row = lax.broadcasted_iota(jnp.int32, (3, 128), 0)
-
-    def output_tile(p, dc):
-        return dot_tn(output_w[p], jnp.where(tap_row == dc, 1.0, 0.0).astype(BF16))
-
-    band(w_output, output_tile, 32, 16, 3, lane_out % 8, 8)
+    tap_row = lax.broadcasted_iota(jnp.int32, (3, 256), 0)
+    tap_lane = lax.broadcasted_iota(jnp.int32, (3, 256), 1) // 64
+    own = jnp.where(tap_row == tap_lane, 1.0, 0.0).astype(BF16)
+    taps = [dot_tn(output_w[p], own) for p in range(3)]
+    for row in range(16):
+        block = jnp.zeros((32, 256), F32)
+        for p in range(3):
+            if 0 <= row - 3 - p < 8:
+                block = block + jnp.where(lane32 % 8 == row - 3 - p, taps[p], 0.0)
+        w_output[32 * row : 32 * row + 32, :] = block.astype(BF16)
     saves[5].start()
 
     wait_bytes(landed2.at[pl.ds(0, 15)], recv_sem.at[1])
@@ -453,11 +500,11 @@
         (2, 16, 256),
         (2, 160, 128),
         (4, 384, 256),
-        (1536, 256),
+        (1024, 256),
         (1152, 256),
-        (1536, 256),
-        (1536, 256),
-        (1536, 128),
+        (1152, 256),
+        (1024, 256),
+        (512, 256),
         (256, 256),
         (256, 256),
     ]
@@ -498,7 +545,7 @@
 
 def network_kernel(*refs):
     sources, (dirty_out, estimate_out), targets = refs[:16], refs[16:18], refs[18:34]
-    window, entry, fine_a, fine_b, fine_c, pooled, coarse, mask, w_pool, drawn, load_sem = refs[34:]
+    window, entry, fine_a, fine_b, fine_c, pooled, coarse, mask, drawn, load_sem = refs[34:]
     loads = [
         pltpu.make_async_copy(source, target, load_sem.at[k])
         for k, (source, target) in enumerate(zip(sources, targets))
@@ -517,10 +564,6 @@
     keep_top = jnp.where(gx == 0, 0.0, 1.0).astype(F32)
     keep_bottom = jnp.where(gx == last_x, 0.0, 1.0).astype(F32)
 
-    rows512 = lax.broadcasted_iota(jnp.int32, (512, 128), 0)
-    lanes512 = lax.broadcasted_iota(jnp.int32, (512, 128), 1)
-    pairs = ((rows512 % 256) // 64 == lanes512 // 32) & (rows512 % 32 == lanes512 % 32)
-    w_pool[...] = jnp.where(pairs, 0.25, 0.0).astype(BF16)
     slab = lax.broadcasted_iota(jnp.int32, (20, 16, 128), 0)
     stripe = lax.broadcasted_iota(jnp.int32, (20, 16, 128), 1)
     col = SLABS * stripe + slab - 9 + 256 * gy
@@ -568,7 +611,7 @@
         entry[q] = placed.astype(BF16)
 
     blank = jnp.zeros((20, 16, 128), BF16)
-    for ref, top in ((fine_a, 37), (fine_b, 37), (fine_c, 37), (pooled, 19), (coarse, 37)):
+    for ref, top in ((fine_a, 37), (fine_b, 37), (fine_c, 37), (pooled, 37), (coarse, 37)):
         ref[0] = blank[: ref.shape[1]]
         ref[top] = blank[: ref.shape[1]]
 
@@ -589,16 +632,28 @@
             value[:, 128 * h : 128 * h + 128].reshape(SLABS, 16, 128) * scaled for h in range(2)
         ]
 
-    def gathered(ref, at, high, slabs, stride, count):
-        pieces = []
-        for dc in range(3):
-            for h in range(high):
-                rows = [
-                    ref[at + stride * g + h, dc : dc + slabs].reshape(slabs * 16, 128)
-                    for g in range(count)
-                ]
-                pieces.append(jnp.concatenate(rows, axis=0))
-        return jnp.concatenate(pieces, axis=1)
+    def beside(ref, group, slabs):
+        lanes = lax.broadcasted_iota(jnp.int32, (slabs, 16, 128), 2)
+        return jnp.where(lanes < 64, ref[2 * group + 3, 0:slabs], ref[2 * group, 0:slabs])
+
+    def gathered(ref, first, count, slabs, pack):
+        columns = [[] for _ in range(8 if pack else 9)]
+        for group in range(count):
+            group = first + group
+            for dc in range(3):
+                for h in range(2):
+                    piece = ref[2 * group + 1 + h, dc : dc + slabs]
+                    columns[2 * dc + h].append(piece.reshape(slabs * 16, 128))
+            edge = beside(ref, group, slabs + 2)
+            edges = [edge[dc : dc + slabs].reshape(slabs * 16, 128) for dc in range(3)]
+            if pack:
+                lanes = lax.broadcasted_iota(jnp.int32, (slabs * 16, 128), 1)
+                turned = jnp.concatenate([edges[0][:, 64:], edges[0][:, :64]], axis=1)
+                middle = (lanes >= 32) & (lanes < 96)
+                edges = [jnp.where(middle, turned, edges[1]), edges[2]]
+            for k, edge in enumerate(edges):
+                columns[6 + k].append(edge)
+        return jnp.concatenate([jnp.concatenate(c, axis=0) for c in columns], axis=1)
 
     arrived(6, 8)
     for variant in range(4):
@@ -613,20 +668,13 @@
                 put(fine_a, 2 * group + 1 + h, value, SLABS)
 
     def encode_step(step, carry):
-        total = dot(gathered(fine_a, 2 * GE * step, 4, SLABS, 2, GE), w_encode[...])
-        columns = [[], [], [], []]
+        total = dot(gathered(fine_a, GE * step, GE, SLABS, True), w_encode[...])
         for g in range(GE):
             group = GE * step + g
             for h, value in enumerate(finish(total[PIX * g : PIX * g + PIX], 1, row_keep(group))):
                 put(fine_b, 2 * group + 1 + h, value, SLABS)
-                split = value.reshape(SLABS // 2, 2, 16, 128)
-                columns[h].append(split[:, 0].reshape(PIX2, 128).astype(BF16))
-                columns[2 + h].append(split[:, 1].reshape(PIX2, 128).astype(BF16))
-        both = jnp.concatenate([jnp.concatenate(c, axis=0) for c in columns], axis=1)
-        small = dot(both, w_pool[...])
-        for g in range(GE):
-            value = small[PIX2 * g : PIX2 * g + PIX2].reshape(SLABS // 2, 16, 128)
-            put(pooled, GE * step + g + 1, value, SLABS // 2)
+                pair = value.reshape(SLABS // 2, 2, 16, 128)
+                put(pooled, 2 * group + 1 + h, (pair[:, 0] + pair[:, 1]) * 0.25, SLABS // 2)
         return carry
 
     arrived(8, 9)
@@ -635,7 +683,7 @@
     even_mask = mask[1:19].reshape(SLABS // 2, 2, 16, 128)[:, 0]
 
     def coarse_step(step, carry):
-        total = dot(gathered(pooled, GC * step, 3, SLABS // 2, 1, GC), w_coarse[...])
+        total = dot(gathered(pooled, GC * step, GC, SLABS // 2, False), w_coarse[...])
         for g in range(GC):
             group = GC * step + g
             value = jnp.maximum(total[PIX2 * g : PIX2 * g + PIX2] + biases[2:3, :], 0.0)
@@ -649,7 +697,7 @@
     lax.fori_loop(0, GROUPS // GC, coarse_step, 0)
 
     def merge_step(step, carry):
-        total = dot(gathered(coarse, 2 * GM * step, 4, SLABS // 2, 2, GM), w_deeper[...])
+        total = dot(gathered(coarse, GM * step, GM, SLABS // 2, False), w_deeper[...])
         value = jnp.maximum(total + biases[3:4, :], 0.0).astype(BF16)
         lifted = dot(value, w_upward[...]).reshape(GM, SLABS // 2, 1, 16, 256)
         halves = []
@@ -671,7 +719,7 @@
     lax.fori_loop(0, GROUPS // GM, merge_step, 0)
 
     def decode_step(step, carry):
-        total = dot(gathered(fine_a, 2 * GD * step, 4, SLABS, 2, GD), w_decode[...])
+        total = dot(gathered(fine_a, GD * step, GD, SLABS, True), w_decode[...])
         for g in range(GD):
             group = GD * step + g
             for h, half in enumerate(finish(total[PIX * g : PIX * g + PIX], 5, row_keep(group))):
@@ -681,21 +729,33 @@
     arrived(13, 14)
     lax.fori_loop(0, GROUPS // GD, decode_step, 0)
 
-    lane_row = lax.broadcasted_iota(jnp.int32, (PIX, 128), 1) // 8
-
-    def output_step(step, carry):
-        total = dot(gathered(fine_c, 2 + 2 * GO * step, 4, SLABS, 2, GO), w_output[...])
-        kept = drawn[...]
-        for g in range(GO):
-            kept = jnp.where(lane_row == GO * step + g, total[PIX * g : PIX * g + PIX], kept)
-        drawn[...] = kept
+    lane_row = lax.broadcasted_iota(jnp.int32, (320, 256), 1) // 8 % 8
+
+    def output_step(half, carry):
+        columns = []
+        for h in range(4):
+            rows = [fine_c[2 * (8 * half + g + 1) + h].reshape(320, 128) for g in range(8)]
+            columns.append(jnp.concatenate(rows, axis=0))
+        total = dot(jnp.concatenate(columns, axis=1), w_output[...])
+        kept = total[0:320]
+        for g in range(1, 8):
+            kept = jnp.where(lane_row == g, total[320 * g : 320 * g + 320], kept)
+        drawn[half] = kept
         return carry
 
-    drawn[...] = jnp.zeros((PIX, 128), F32)
     arrived(14, 16)
-    lax.fori_loop(0, 16 // GO, output_step, 0)
-
-    update = drawn[...]
+    lax.fori_loop(0, 2, output_step, 0)
+
+    sums = []
+    for half in range(2):
+        taps = drawn[half].reshape(20, 16, 256)
+        left = taps[0:18, :, 0:128] + taps[2:20, :, 128:256]
+        middle = taps[1:19, :, 0:128].reshape(PIX, 128)
+        sums.append((left.reshape(PIX, 128), pltpu.roll(middle, 64, 1)))
+    lanes = lax.broadcasted_iota(jnp.int32, (PIX, 128), 1)
+    upper = sums[0][0] + sums[0][1]
+    lower = pltpu.roll(sums[1][0] + sums[1][1], 64, 1)
+    update = jnp.where(lanes < 64, upper, lower)
     high = update.astype(BF16)
     low = (update - high.astype(F32)).astype(BF16)
     ordered = dot(back[...], high) + dot(back[...], low)
@@ -724,11 +784,10 @@
             pltpu.VMEM((38, 20, 16, 128), BF16),
             pltpu.VMEM((38, 20, 16, 128), BF16),
             pltpu.VMEM((38, 20, 16, 128), BF16),
-            pltpu.VMEM((20, 11, 16, 128), BF16),
+            pltpu.VMEM((38, 11, 16, 128), BF16),
             pltpu.VMEM((38, 11, 16, 128), BF16),
             pltpu.VMEM((20, 16, 128), F32),
-            pltpu.VMEM((512, 128), BF16),
-            pltpu.VMEM((PIX, 128), F32),
+            pltpu.VMEM((2, 320, 256), F32),
             pltpu.SemaphoreType.DMA((len(operands),)),
         ],
         compiler_params=pltpu.CompilerParams(vmem_limit_bytes=64 << 20),

time: 85.3 us -> 76.4 us (0.90)
  Pallas kernels: 84.6 us -> 75.4 us
    pallas_call x1, Pallas kernels: 27.5 us -> 19.9 us  [network(): pl.pallas_call(network_kernel, out_shape=(jax.ShapeDtypeStruct((128, 256)...]
    pallas_call x1, Pallas kernels: 57 us -> 55.5 us  [exchange(): pl.pallas_call(exchange_kernel, out_shape=tuple(outs), in_specs=[hbm] * l...]
where the time goes in v3:
time: 76.4 us; the launch traced here: 76.3 us
  Pallas kernels  75.4 us (99%)
  between operations  0.81 us (1%)
    pallas_call x1, Pallas kernels, exchange(): pl.pallas_call(exchange_kernel, out_shape=tuple(outs), in_specs=[hbm] * l...  55.5 us
    pallas_call x1, Pallas kernels, network(): pl.pallas_call(network_kernel, out_shape=(jax.ShapeDtypeStruct((128, 256)...  19.9 us

profile of v3, /device:TPU:1, one launch (start us, length us, event | category | flops | bytes accessed | tf_op | source)
XLA Modules:
  0.0 76.3 jit_solution(8096524834127869622)
XLA Ops:
  0.6 55.5 %exchange.1 = (bf16[34,16,128]{2,1,0:T(8,128)(2,1)}, bf16[2,16,256]{2,1,0:T(8,128)(2,1)}, bf16[2,160,128]{2,1,0:T(8,128)(2,1)}, bf16[4,384,256]{2,1,0:T(8,128)(2...) custom-call(bf16[256,256]{1,0:T(8,128)(2,1)} %constant.18.clone.refs, ...), custom_call_target="tpu_custom_call" | custom-call | tf_op jit(solution)/shard_map/exchange/pallas_call | solution.py:513
  56.2 19.9 %network.1 = (f32[128,256]{1,0:T(8,128)}, f32[128,256]{1,0:T(8,128)}) custom-call(f32[128,256]{1,0:T(8,128)} %refs_0_.2, bf16[34,16,128]{2,1,0:T(8,128)(2,1)} %get-tuple-element.14.refs_1_, bf16[2,16,256]{2,1,0:T(8,128)(2,1)} %get-tuple-element.15.refs_2_, bf16[2,160,128]{2,1,0:T(8,128)(2,1)} %get-tuple-element.16.refs_3_, ...), custom_call_target="tpu_custom_call" | custom-call | tf_op jit(solution)/shard_map/network/pallas_call | solution.py:772

commit v4 on v3

--- a/solution.py
+++ b/solution.py
@@ -13,7 +13,7 @@
 F32 = jnp.float32
 BF16 = jnp.bfloat16
 
-GE, GC, GM, GD = 9, 9, 9, 9
+GE, GC, GM, GN, GD = 9, 9, 9, 9, 9
 NX, NY = 32, 16
 SLABS = 18
 STRIPES = 16
@@ -81,11 +81,15 @@
     return jnp.asarray(into.reshape(320, 384), BF16), jnp.asarray(back.reshape(256, PIX), BF16)
 
 
+def farthest_first(step, count, me):
+    away = (step + 1) // 2
+    shift = count // 2 + jnp.where(step % 2 == 1, away, -away)
+    return lax.rem(me + shift, count)
+
+
 def send_all(axis, count, me, source, landing, send_sem, recv_sem):
     def one(step, carry):
-        away = (step + 1) // 2
-        shift = count // 2 + jnp.where(step % 2 == 1, away, -away)
-        other = lax.rem(me + shift, count)
+        other = farthest_first(step, count, me)
         pltpu.make_async_remote_copy(
             src_ref=source.at[other],
             dst_ref=landing.at[me],
@@ -229,7 +233,7 @@
     ) = refs[:12]
     weights_h = refs[12:26]
     dirty_out, rows_out, cols_out = refs[26:29]
-    bands_out = refs[29:38]
+    bands_out = refs[29:37]
     (
         first,
         twist1,
@@ -243,10 +247,10 @@
         counts,
         owner,
         sky,
-    ) = refs[38:50]
-    weights = refs[50:64]
-    built = refs[64:73]
-    w_enter, w_encode, w_coarse, w_deeper, w_decode, w_output, w_upward, w_skip, biases = built
+    ) = refs[37:49]
+    weights = refs[49:63]
+    built = refs[63:71]
+    w_enter, w_encode, w_coarse, w_deeper, w_decode, w_output, w_merge, biases = built
     (
         tiles,
         landed1,
@@ -266,15 +270,15 @@
         recv_sem,
         load_sem,
         save_sem,
-    ) = refs[73:]
+    ) = refs[71:]
     saves = [
         pltpu.make_async_copy(source, target, save_sem.at[k])
         for k, (source, target) in enumerate(zip(built, bands_out))
     ]
-    save_rows = pltpu.make_async_copy(sky_rows, rows_out, save_sem.at[9])
-    save_cols = pltpu.make_async_copy(sky_sides, cols_out, save_sem.at[10])
-    save_main = pltpu.make_async_copy(landed4, dirty_out.at[pl.ds(0, 32)], save_sem.at[11])
-    save_sides = pltpu.make_async_copy(sides, dirty_out.at[pl.ds(32, 2)], save_sem.at[12])
+    save_rows = pltpu.make_async_copy(sky_rows, rows_out, save_sem.at[8])
+    save_cols = pltpu.make_async_copy(sky_sides, cols_out, save_sem.at[9])
+    save_main = pltpu.make_async_copy(landed4, dirty_out.at[pl.ds(0, 32)], save_sem.at[10])
+    save_sides = pltpu.make_async_copy(sides, dirty_out.at[pl.ds(32, 2)], save_sem.at[11])
     gx, gy = lax.axis_index("gx"), lax.axis_index("gy")
     down_x, up_x = lax.rem(gx + 1, NX), lax.rem(gx + NX - 1, NX)
     right_y, left_y = lax.rem(gy + 1, NY), lax.rem(gy + NY - 1, NY)
@@ -282,12 +286,11 @@
 
     def greet(axis, count, me):
         def one(step, carry):
-            pl.semaphore_signal(
-                barrier, inc=1, device_id={axis: lax.rem(me + step, count)}, device_id_type=MESH
-            )
+            other = farthest_first(step, count, me)
+            pl.semaphore_signal(barrier, inc=1, device_id={axis: other}, device_id_type=MESH)
             return carry
 
-        lax.fori_loop(1, count, one, 0)
+        lax.fori_loop(0, count - 1, one, 0)
 
     greet("gy", NY, gy)
     greet("gx", NX, gx)
@@ -358,11 +361,13 @@
 
     for copy in row_copies:
         copy.wait()
-    for half in range(2):
+    above, below = sky_rows[0].astype(F32)[8:16], sky_rows[1].astype(F32)[0:8]
+    outer_rows = jnp.concatenate([below, jnp.zeros((112, 256), F32), above], axis=0).astype(BF16)
+    for half, chosen, at in ((0, eye[0:16], 0), (1, eye[112:128], 8)):
         lanes = slice(128 * half, 128 * half + 128)
-        sky_cols[half, 0:16] = sky_rows[0, :, lanes]
-        sky_cols[half, 16:144] = sky_own[:, lanes]
-        sky_cols[half, 144:160] = sky_rows[1, :, lanes]
+        both = [dot_nt(chosen, sky_own[:, lanes]), dot_nt(chosen, outer_rows[:, lanes])]
+        both = [part[at : at + 8] for part in both]
+        sky_cols[half] = jnp.concatenate(both, axis=0).astype(BF16)
     col_copies = [
         to_side(sky_cols.at[1], sky_sides.at[0], 6, "gy", right_y),
         to_side(sky_cols.at[0], sky_sides.at[1], 7, "gy", left_y),
@@ -406,11 +411,11 @@
     lifted = dot_tn(upward_w[...], rep32)
     for row in range(4):
         block = jnp.where(lane64 // 64 == row, lifted, 0.0)
-        w_upward[64 * row : 64 * row + 64, :] = block.astype(BF16)
+        w_merge[256 + 64 * row : 320 + 64 * row, :] = block.astype(BF16)
     skipped = dot_tn(skip_w[...], rep32)
     for row in range(8):
         block = jnp.where(lane32 // 32 == row, skipped, 0.0)
-        w_skip[32 * row : 32 * row + 32, :] = block.astype(BF16)
+        w_merge[32 * row : 32 * row + 32, :] = block.astype(BF16)
     row_id = lax.broadcasted_iota(jnp.int32, (64, 256), 0)
     for dc in range(3):
         taps = [dot(enter_w[p, dc], rep32) for p in range(3)]
@@ -425,7 +430,7 @@
     for row, ref in enumerate(weights[8:]):
         biases[row : row + 1, :] = jnp.concatenate([ref[...]] * (256 // ref.shape[1]), axis=1)
     biases[6:8, :] = jnp.zeros((2, 256), F32)
-    for k in (0, 6, 7, 8):
+    for k in (0, 6, 7):
         saves[k].start()
 
     def store(y, value):
@@ -498,15 +503,14 @@
     shapes = [
         (34, 16, 128),
         (2, 16, 256),
-        (2, 160, 128),
+        (2, 16, 128),
         (4, 384, 256),
         (1024, 256),
         (1152, 256),
         (1152, 256),
         (1024, 256),
         (512, 256),
-        (256, 256),
-        (256, 256),
+        (512, 256),
     ]
     outs = [jax.ShapeDtypeStruct(shape, BF16) for shape in shapes]
     outs.append(jax.ShapeDtypeStruct((8, 256), F32))
@@ -528,13 +532,13 @@
             pltpu.VMEM((32, 16, 128), BF16),
             pltpu.VMEM((2, 16, 128), BF16),
             pltpu.VMEM((2, 16, 256), BF16),
-            pltpu.VMEM((2, 160, 128), BF16),
-            pltpu.VMEM((2, 160, 128), BF16),
+            pltpu.VMEM((2, 16, 128), BF16),
+            pltpu.VMEM((2, 16, 128), BF16),
             pltpu.VMEM((128, 256), BF16),
             pltpu.SemaphoreType.DMA((10,)),
             pltpu.SemaphoreType.DMA((10,)),
             pltpu.SemaphoreType.DMA((len(operands),)),
-            pltpu.SemaphoreType.DMA((13,)),
+            pltpu.SemaphoreType.DMA((12,)),
         ],
         compiler_params=pltpu.CompilerParams(
             collective_id=0, has_side_effects=True, vmem_limit_bytes=64 << 20
@@ -544,8 +548,9 @@
 
 
 def network_kernel(*refs):
-    sources, (dirty_out, estimate_out), targets = refs[:16], refs[16:18], refs[18:34]
-    window, entry, fine_a, fine_b, fine_c, pooled, coarse, mask, drawn, load_sem = refs[34:]
+    sources, (dirty_hbm, estimate_out), targets = refs[:15], refs[15:17], refs[17:32]
+    window, entry, fine_a, fine_b, fine_c, pooled, coarse, deep, mask, drawn, dirty_out, load_sem = refs[32:]
+    save_dirty = pltpu.make_async_copy(dirty_out, dirty_hbm, load_sem.at[15])
     loads = [
         pltpu.make_async_copy(source, target, load_sem.at[k])
         for k, (source, target) in enumerate(zip(sources, targets))
@@ -553,7 +558,7 @@
     for load in loads:
         load.start()
     sky, dirty_in, rows_in, cols_in, eye, into, w_enter, biases = targets[:8]
-    w_encode, w_coarse, w_deeper, w_upward, w_skip, w_decode, w_output, back = targets[8:]
+    w_encode, w_coarse, w_deeper, w_merge, w_decode, w_output, back = targets[8:]
 
     def arrived(first, last):
         for load in loads[first:last]:
@@ -570,45 +575,36 @@
     mask[...] = jnp.where((col >= 0) & (col < 256 * (last_y + 1)), 1.0, 0.0).astype(F32)
 
     arrived(0, 6)
-    lane = lax.broadcasted_iota(jnp.int32, (160, 128), 1)
-    beside = jnp.where(lane < 64, cols_in[1].astype(F32), cols_in[0].astype(F32))
     above = rows_in[0].astype(F32)[8:16] * keep_top
     below = rows_in[1].astype(F32)[0:8] * keep_bottom
-    zeros = jnp.zeros((32, 256), F32)
+    zeros = jnp.zeros((32, 512), F32)
     window[0, :, 0:256] = jnp.concatenate(
-        [zeros[:16], above, sky[...], below, zeros], axis=0
+        [zeros[:16, :256], above, sky[...], below, zeros[:, :256]], axis=0
     ).astype(BF16)
-    beside = jnp.concatenate(
-        [
-            zeros[:16, :128],
-            beside[8:16] * keep_top,
-            beside[16:144],
-            beside[144:152] * keep_bottom,
-            zeros[:, :128],
-        ],
-        axis=0,
-    )
-    window[0, :, 256:384] = beside.astype(BF16)
-    wide = dirty_in[...].astype(F32)
+    wide, sides = dirty_in[...].astype(F32), cols_in[...].astype(F32)
     gap = jnp.zeros((112, 128), F32)
     parts = []
     for half in range(2):
         rows8 = slice(8 * half, 8 * half + 8)
-        stacked = jnp.concatenate(
-            [wide[0:32, rows8].reshape(256, 128), wide[33, rows8], gap, wide[32, rows8]], axis=0
-        )
-        parts.append(dot_nt(eye[...], stacked.astype(BF16)))
+        stacked = [wide[0:32, rows8].reshape(256, 128), wide[33, rows8], gap, wide[32, rows8]]
+        stacked += [sides[1, rows8], gap, sides[0, rows8]]
+        parts.append(dot_nt(eye[...], jnp.concatenate(stacked, axis=0).astype(BF16)))
     dirty_out[...] = parts[0][:, 0:256]
-    zeros = jnp.zeros((32, 384), F32)
-    window[1] = jnp.concatenate(
+    save_dirty.start()
+    whole = jnp.concatenate(
         [zeros[:16], parts[1][120:128] * keep_top, parts[0], parts[1][0:8] * keep_bottom, zeros],
         axis=0,
     ).astype(BF16)
+    window[1] = whole[:, 0:384]
+    window[0, :, 256:384] = whole[:, 384:512]
+    pieces = []
     for q in range(5):
         rows64 = slice(32 * q, 32 * q + 64)
-        both = jnp.concatenate([window[0, rows64], window[1, rows64]], axis=0)
-        placed = dot_nt(into[...], both).reshape(20, 16, 128) * mask[...]
-        entry[q] = placed.astype(BF16)
+        pieces += [window[0, rows64], window[1, rows64]]
+    placed = dot_nt(into[...], jnp.concatenate(pieces, axis=0))
+    for q in range(5):
+        value = placed[:, 128 * q : 128 * q + 128].reshape(20, 16, 128) * mask[...]
+        entry[q] = value.astype(BF16)
 
     blank = jnp.zeros((20, 16, 128), BF16)
     for ref, top in ((fine_a, 37), (fine_b, 37), (fine_c, 37), (pooled, 37), (coarse, 37)):
@@ -696,27 +692,41 @@
     arrived(9, 10)
     lax.fori_loop(0, GROUPS // GC, coarse_step, 0)
 
-    def merge_step(step, carry):
+    def deeper_step(step, carry):
         total = dot(gathered(coarse, GM * step, GM, SLABS // 2, False), w_deeper[...])
         value = jnp.maximum(total + biases[3:4, :], 0.0).astype(BF16)
-        lifted = dot(value, w_upward[...]).reshape(GM, SLABS // 2, 1, 16, 256)
-        halves = []
+        for g in range(GM):
+            piece = value[PIX2 * g : PIX2 * g + PIX2].reshape(SLABS // 2, 16, 256)
+            for h in range(2):
+                deep[2 * (GM * step + g) + h] = piece[:, :, 128 * h : 128 * h + 128]
+        return carry
+
+    arrived(10, 11)
+    lax.fori_loop(0, GROUPS // GM, deeper_step, 0)
+
+    def merge_step(step, carry):
+        columns = []
         for h in range(2):
             rows = [
-                fine_b[2 * (GM * step + g) + 1 + h, 1:19].reshape(PIX, 128) for g in range(GM)
+                fine_b[2 * (GN * step + g) + 1 + h, 1:19].reshape(PIX, 128) for g in range(GN)
             ]
-            halves.append(jnp.concatenate(rows, axis=0))
-        skipped = dot(jnp.concatenate(halves, axis=1), w_skip[...])
-        total = skipped.reshape(GM, SLABS // 2, 2, 16, 256) + lifted
-        total = total.reshape(GM * PIX, 256)
-        for g in range(GM):
-            group = GM * step + g
+            columns.append(jnp.concatenate(rows, axis=0))
+        for h in range(2):
+            rows = []
+            for g in range(GN):
+                low = deep[2 * (GN * step + g) + h].reshape(SLABS // 2, 1, 16, 128)
+                low = jnp.broadcast_to(low, (SLABS // 2, 2, 16, 128))
+                rows.append(low.reshape(PIX, 128))
+            columns.append(jnp.concatenate(rows, axis=0))
+        total = dot(jnp.concatenate(columns, axis=1), w_merge[...])
+        for g in range(GN):
+            group = GN * step + g
             for h, half in enumerate(finish(total[PIX * g : PIX * g + PIX], 4, row_keep(group))):
                 put(fine_a, 2 * group + 1 + h, half, SLABS)
         return carry
 
-    arrived(10, 13)
-    lax.fori_loop(0, GROUPS // GM, merge_step, 0)
+    arrived(11, 12)
+    lax.fori_loop(0, GROUPS // GN, merge_step, 0)
 
     def decode_step(step, carry):
         total = dot(gathered(fine_a, GD * step, GD, SLABS, True), w_decode[...])
@@ -726,7 +736,7 @@
                 put(fine_c, 2 * group + 1 + h, half, SLABS)
         return carry
 
-    arrived(13, 14)
+    arrived(12, 13)
     lax.fori_loop(0, GROUPS // GD, decode_step, 0)
 
     lane_row = lax.broadcasted_iota(jnp.int32, (320, 256), 1) // 8 % 8
@@ -743,7 +753,7 @@
         drawn[half] = kept
         return carry
 
-    arrived(14, 16)
+    arrived(13, 15)
     lax.fori_loop(0, 2, output_step, 0)
 
     sums = []
@@ -760,15 +770,16 @@
     low = (update - high.astype(F32)).astype(BF16)
     ordered = dot(back[...], high) + dot(back[...], low)
     estimate_out[...] = sky[...] + ordered.T
+    save_dirty.wait()
 
 
 def network(sky, dirty_in, rows_in, cols_in, bands):
     vmem, hbm = pl.BlockSpec(memory_space=pltpu.VMEM), pl.BlockSpec(memory_space=pltpu.HBM)
     into, back = permutations()
     eye = jnp.asarray(np.eye(128), BF16)
-    enter, encode, coarse, deeper, decode, output, upward, skip, biases = bands
+    enter, encode, coarse, deeper, decode, output, merge, biases = bands
     operands = (sky, dirty_in, rows_in, cols_in, eye, into, enter, biases)
-    operands += (encode, coarse, deeper, upward, skip, decode, output, back)
+    operands += (encode, coarse, deeper, merge, decode, output, back)
     return pl.pallas_call(
         network_kernel,
         out_shape=(
@@ -776,7 +787,7 @@
             jax.ShapeDtypeStruct((128, 256), F32),
         ),
         in_specs=[hbm] * len(operands),
-        out_specs=(vmem, vmem),
+        out_specs=(hbm, vmem),
         scratch_shapes=[pltpu.VMEM(x.shape, x.dtype) for x in operands]
         + [
             pltpu.VMEM((2, 192, 384), BF16),
@@ -786,9 +797,11 @@
             pltpu.VMEM((38, 20, 16, 128), BF16),
             pltpu.VMEM((38, 11, 16, 128), BF16),
             pltpu.VMEM((38, 11, 16, 128), BF16),
+            pltpu.VMEM((36, 9, 16, 128), BF16),
             pltpu.VMEM((20, 16, 128), F32),
             pltpu.VMEM((2, 320, 256), F32),
-            pltpu.SemaphoreType.DMA((len(operands),)),
+            pltpu.VMEM((128, 256), F32),
+            pltpu.SemaphoreType.DMA((len(operands) + 1,)),
         ],
         compiler_params=pltpu.CompilerParams(vmem_limit_bytes=64 << 20),
         name="network",

time: 76.4 us -> 74.2 us (0.971)
  Pallas kernels: 75.4 us -> 73.4 us
    pallas_call x1, Pallas kernels: 55.5 us -> 54.2 us  [exchange(): pl.pallas_call(exchange_kernel, out_shape=tuple(outs), in_specs=[hbm] * l...]
where the time goes in v4:
time: 74.2 us; the launch traced here: 74.1 us
  Pallas kernels  73.4 us (99%)
    pallas_call x1, Pallas kernels, exchange(): pl.pallas_call(exchange_kernel, out_shape=tuple(outs), in_specs=[hbm] * l...  54.2 us
    pallas_call x1, Pallas kernels, network(): pl.pallas_call(network_kernel, out_shape=(jax.ShapeDtypeStruct((128, 256)...  19.2 us

profile of v4, /device:TPU:1, one launch (start us, length us, event | category | flops | bytes accessed | tf_op | source)
XLA Modules:
  0.0 74.1 jit_solution(37483548177325711)
XLA Ops:
  0.6 54.2 %exchange.1 = (bf16[34,16,128]{2,1,0:T(8,128)(2,1)}, bf16[2,16,256]{2,1,0:T(8,128)(2,1)}, bf16[2,16,128]{2,1,0:T(8,128)(2,1)}, bf16[4,384,256]{2,1,0:T(8,128)(2,...) custom-call(bf16[256,256]{1,0:T(8,128)(2,1)} %constant.18.clone.refs, ...), custom_call_target="tpu_custom_call" | custom-call | tf_op jit(solution)/shard_map/exchange/pallas_call | solution.py:517
  54.9 19.2 %network.1 = (f32[128,256]{1,0:T(8,128)}, f32[128,256]{1,0:T(8,128)}) custom-call(f32[128,256]{1,0:T(8,128)} %refs_0_.2, bf16[34,16,128]{2,1,0:T(8,128)(2,1)} %get-tuple-element.13.refs_1_, bf16[2,16,256]{2,1,0:T(8,128)(2,1)} %get-tuple-element.14.refs_2_, bf16[2,16,128]{2,1,0:T(8,128)(2,1)} %get-tuple-element.15.refs_3_, ...), custom_call_target="tpu_custom_call" | custom-call | tf_op jit(solution)/shard_map/network/pallas_call | solution.py:783

commit v5 on v4

--- a/solution.py
+++ b/solution.py
@@ -13,7 +13,7 @@
 F32 = jnp.float32
 BF16 = jnp.bfloat16
 
-GE, GC, GM, GN, GD = 9, 9, 9, 9, 9
+GE, GC, GM, GN, GD = 9, 18, 9, 9, 9
 NX, NY = 32, 16
 SLABS = 18
 STRIPES = 16
@@ -574,6 +574,11 @@
     col = SLABS * stripe + slab - 9 + 256 * gy
     mask[...] = jnp.where((col >= 0) & (col < 256 * (last_y + 1)), 1.0, 0.0).astype(F32)
 
+    blank = jnp.zeros((20, 16, 128), BF16)
+    for ref, top in ((fine_a, 37), (fine_b, 37), (fine_c, 37), (pooled, 37), (coarse, 37)):
+        ref[0] = blank[: ref.shape[1]]
+        ref[top] = blank[: ref.shape[1]]
+
     arrived(0, 6)
     above = rows_in[0].astype(F32)[8:16] * keep_top
     below = rows_in[1].astype(F32)[0:8] * keep_bottom
@@ -606,11 +611,6 @@
         value = placed[:, 128 * q : 128 * q + 128].reshape(20, 16, 128) * mask[...]
         entry[q] = value.astype(BF16)
 
-    blank = jnp.zeros((20, 16, 128), BF16)
-    for ref, top in ((fine_a, 37), (fine_b, 37), (fine_c, 37), (pooled, 37), (coarse, 37)):
-        ref[0] = blank[: ref.shape[1]]
-        ref[top] = blank[: ref.shape[1]]
-
     def row_keep(group):
         top = jnp.where(group == 0, keep_top, 1.0)
         bottom = jnp.where(group == GROUPS - 1, keep_bottom, 1.0)
@@ -623,7 +623,7 @@
 
     def finish(total, bias_row, keep):
         value = jnp.maximum(total + biases[bias_row : bias_row + 1, :], 0.0)
-        scaled = mask[1:19] * keep
+        scaled = mask[1:19] if keep is None else mask[1:19] * keep
         return [
             value[:, 128 * h : 128 * h + 128].reshape(SLABS, 16, 128) * scaled for h in range(2)
         ]
@@ -660,14 +660,16 @@
             pieces.append(jnp.concatenate(rows, axis=0))
         total = dot(jnp.concatenate(pieces, axis=1), w_enter[variant])
         for g, group in enumerate(members):
-            for h, value in enumerate(finish(total[PIX * g : PIX * g + PIX], 0, row_keep(group))):
+            keep = row_keep(group) if group in (0, GROUPS - 1) else None
+            for h, value in enumerate(finish(total[PIX * g : PIX * g + PIX], 0, keep)):
                 put(fine_a, 2 * group + 1 + h, value, SLABS)
 
     def encode_step(step, carry):
         total = dot(gathered(fine_a, GE * step, GE, SLABS, True), w_encode[...])
         for g in range(GE):
             group = GE * step + g
-            for h, value in enumerate(finish(total[PIX * g : PIX * g + PIX], 1, row_keep(group))):
+            keep = row_keep(group) if g in (0, GE - 1) else None
+            for h, value in enumerate(finish(total[PIX * g : PIX * g + PIX], 1, keep)):
                 put(fine_b, 2 * group + 1 + h, value, SLABS)
                 pair = value.reshape(SLABS // 2, 2, 16, 128)
                 put(pooled, 2 * group + 1 + h, (pair[:, 0] + pair[:, 1]) * 0.25, SLABS // 2)
@@ -683,7 +685,7 @@
         for g in range(GC):
             group = GC * step + g
             value = jnp.maximum(total[PIX2 * g : PIX2 * g + PIX2] + biases[2:3, :], 0.0)
-            scaled = even_mask * row_keep(group)
+            scaled = even_mask * row_keep(group) if g in (0, GC - 1) else even_mask
             for h in range(2):
                 half = value[:, 128 * h : 128 * h + 128].reshape(SLABS // 2, 16, 128) * scaled
                 put(coarse, 2 * group + 1 + h, half, SLABS // 2)
@@ -721,7 +723,8 @@
         total = dot(jnp.concatenate(columns, axis=1), w_merge[...])
         for g in range(GN):
             group = GN * step + g
-            for h, half in enumerate(finish(total[PIX * g : PIX * g + PIX], 4, row_keep(group))):
+            keep = row_keep(group) if g in (0, GN - 1) else None
+            for h, half in enumerate(finish(total[PIX * g : PIX * g + PIX], 4, keep)):
                 put(fine_a, 2 * group + 1 + h, half, SLABS)
         return carry
 
@@ -732,7 +735,8 @@
         total = dot(gathered(fine_a, GD * step, GD, SLABS, True), w_decode[...])
         for g in range(GD):
             group = GD * step + g
-            for h, half in enumerate(finish(total[PIX * g : PIX * g + PIX], 5, row_keep(group))):
+            keep = row_keep(group) if g in (0, GD - 1) else None
+            for h, half in enumerate(finish(total[PIX * g : PIX * g + PIX], 5, keep)):
                 put(fine_c, 2 * group + 1 + h, half, SLABS)
         return carry
 

time: 74.2 us -> 74 us (level)
  no operation moved by 1% of the time
where the time goes in v5:
time: 74 us; the launch traced here: 73.9 us
  Pallas kernels  73.1 us (99%)
  between operations  0.81 us (1%)
    pallas_call x1, Pallas kernels, exchange(): pl.pallas_call(exchange_kernel, out_shape=tuple(outs), in_specs=[hbm] * l...  54.2 us
    pallas_call x1, Pallas kernels, network(): pl.pallas_call(network_kernel, out_shape=(jax.ShapeDtypeStruct((128, 256)...  18.9 us

profile of v5, /device:TPU:1, one launch (start us, length us, event | category | flops | bytes accessed | tf_op | source)
XLA Modules:
  0.0 73.9 jit_solution(17297356266815540389)
XLA Ops:
  0.6 54.2 %exchange.1 = (bf16[34,16,128]{2,1,0:T(8,128)(2,1)}, bf16[2,16,256]{2,1,0:T(8,128)(2,1)}, bf16[2,16,128]{2,1,0:T(8,128)(2,1)}, bf16[4,384,256]{2,1,0:T(8,128)(2,...) custom-call(bf16[256,256]{1,0:T(8,128)(2,1)} %constant.18.clone.refs, ...), custom_call_target="tpu_custom_call" | custom-call | tf_op jit(solution)/shard_map/exchange/pallas_call | solution.py:517
  54.8 18.9 %network.1 = (f32[128,256]{1,0:T(8,128)}, f32[128,256]{1,0:T(8,128)}) custom-call(f32[128,256]{1,0:T(8,128)} %refs_0_.2, bf16[34,16,128]{2,1,0:T(8,128)(2,1)} %get-tuple-element.13.refs_1_, bf16[2,16,256]{2,1,0:T(8,128)(2,1)} %get-tuple-element.14.refs_2_, bf16[2,16,128]{2,1,0:T(8,128)(2,1)} %get-tuple-element.15.refs_3_, ...), custom_call_target="tpu_custom_call" | custom-call | tf_op jit(solution)/shard_map/network/pallas_call | solution.py:787
